TPU v7x, 256 devices: a whole 4x4x8 slice. The times are simulated.
256 devices in a mesh: heads: 8 (over x, core), seq: 32 (over y, z).
Axes of the slice: x: 4, y: 4, z: 8, core: 2. Of those that a mesh axis runs over, the one named last changes fastest.
Arguments:
- tokens: bfloat16 [8192, 4096], P('seq'), may hold values from -6 to 6
- norm_gain: float32 [4096], replicated, may hold values from 0.1 to 1.9
- w_query: bfloat16 [4096, 4096], P(None, 'heads'), may hold values from -0.09375 to 0.09375
- w_key: bfloat16 [4096, 1024], P(None, 'heads'), may hold values from -0.1875 to 0.1875
- w_value: bfloat16 [4096, 1024], P(None, 'heads'), may hold values from -0.375 to 0.375
- w_out: bfloat16 [4096, 4096], P('heads'), may hold values from -0.09375 to 0.09375
- cache_keys: bfloat16 [8, 32768, 128], P('heads', 'seq'), may hold values from -360 to 360
- cache_values: bfloat16 [8, 32768, 128], P('heads', 'seq'), may hold values from -24 to 24
- vert_blocks: int32 [8, 64], P('heads'), may hold values from -1 to 511, as said below
- vert_count: int32 [8], P('heads'), may hold values from 32 to 64
- slash_offsets: int32 [8, 4], P('heads'), may hold values from -1 to 4, as said below
- slash_count: int32 [8], P('heads'), may hold values from 1 to 4
Outputs:
- layer_out: bfloat16 [8192, 4096], P('seq', 'heads')
Inputs may be any that keep to these rules, and one draw needn't show every extreme that they name: `vert_blocks`: row g lists cache blocks for key/value head g: its entries before vert_count[g] are distinct, the rest are -1. The cache of one index of seq holds at most 8 of the blocks that a row lists, and exactly 8 for one index in every row. `slash_offsets`: entries of row g before slash_count[g] are distinct, the rest are -1.
All inputs are finite; a program needn't handle non-finite values.
Results may differ from a plain program's by a relative error of at most 0.015.
The roundings to bfloat16 on the way count: a program that leaves them out, or rounds other values in their place, can miss the bound.
Values may be sent and summed in bfloat16 or wider, within the bound.
No kernel may reach another device: no remote copies, remote signals or barrier semaphores. Data moves between devices by JAX's collectives and lax.ppermute only.
A program may use at most 64 MiB of HBM per device.

v0:
```python
import math

import jax
import jax.numpy as jnp
from jax import lax
from jax.sharding import PartitionSpec as P

BLK = 64
VCAP = 8


def passed_along(block, axis, distance):
    devices = range(lax.axis_size(axis))
    route = [(i - distance, i) for i in devices if i - distance in devices]
    return lax.ppermute(block, axis, route)


def attend_slots(carried, kv_slots, slot_flags, head_queries, score_scale):
    slot_total = kv_slots.shape[0]
    block_len = kv_slots.shape[3]
    slot_group = 1
    for candidate in (32, 16, 8, 4, 2):
        slot_group = candidate
        break
    groups = slot_total // slot_group
    stacked = kv_slots.reshape((groups, slot_group) + kv_slots.shape[1:])
    grouped_flags = slot_flags.reshape(groups, slot_group, slot_flags.shape[1])

    def fold_step(running, entry):
        running_max, running_sum, accumulate = running
        kv_block, slot_ok = entry
        scores = (
            jnp.einsum(
                "krh,sknh->krsn",
                head_queries,
                kv_block[:, :, 0],
                preferred_element_type=jnp.float32,
            )
            * score_scale
        )
        scores = jnp.where(slot_ok.T[:, None, :, None], scores, -jnp.inf)
        scores = scores.reshape(scores.shape[0], scores.shape[1], -1)
        new_max = jnp.maximum(running_max, jnp.max(scores, axis=-1))
        factor = jnp.exp(running_max - new_max)
        weights = jnp.exp(scores - new_max[..., None])
        running_sum = running_sum * factor + jnp.sum(weights, axis=-1)
        rounded = weights.astype(jnp.bfloat16).reshape(
            weights.shape[0], weights.shape[1], slot_group, block_len
        )
        accumulate = accumulate * factor[..., None] + jnp.einsum(
            "krsn,sknh->krh", rounded, kv_block[:, :, 1], preferred_element_type=jnp.float32
        )
        return ((new_max, running_sum, accumulate), None)

    result, _ = lax.scan(fold_step, carried, (stacked, grouped_flags))
    return result


def local(
    tokens,
    norm_gain,
    w_query,
    w_key,
    w_value,
    w_out,
    cache_keys,
    cache_values,
    vert_blocks,
    vert_count,
    slash_offsets,
    slash_count,
):
    local_heads = cache_keys.shape[0]
    head_dim = cache_keys.shape[2]
    tok_rows = tokens.shape[0]
    group_size = w_query.shape[1] // (local_heads * head_dim)
    score_scale = 1.0 / math.sqrt(head_dim)
    seq_index = lax.axis_index("seq")
    activation = tokens.astype(jnp.float32)
    normed = (
        activation
        * lax.rsqrt(jnp.mean(activation * activation, axis=-1, keepdims=True) + 1e-05)
        * norm_gain
    ).astype(jnp.bfloat16)
    queries = jnp.dot(normed, w_query, preferred_element_type=jnp.float32).astype(jnp.bfloat16)
    key_rows = jnp.dot(normed, w_key, preferred_element_type=jnp.float32).astype(jnp.bfloat16)
    value_rows = jnp.dot(normed, w_value, preferred_element_type=jnp.float32).astype(jnp.bfloat16)
    head_queries = (
        queries.reshape(tok_rows, local_heads, group_size, head_dim)
        .transpose(1, 2, 0, 3)
        .reshape(local_heads, group_size * tok_rows, head_dim)
    )
    before_keys, before_values = passed_along((key_rows, value_rows), "seq", 1)
    prev_rows = before_keys.shape[0]
    near_keys = jnp.concatenate([before_keys, key_rows], 0).reshape(
        prev_rows + tok_rows, local_heads, head_dim
    )
    near_values = jnp.concatenate([before_values, value_rows], 0).reshape(
        prev_rows + tok_rows, local_heads, head_dim
    )
    scores = (
        jnp.einsum("krh,nkh->krn", head_queries, near_keys, preferred_element_type=jnp.float32)
        * score_scale
    )
    scores = scores.reshape(local_heads, group_size, tok_rows, prev_rows + tok_rows)
    row_index = jnp.arange(tok_rows)[:, None]
    key_index = jnp.arange(prev_rows + tok_rows)[None, :] - prev_rows
    block_gap = row_index // BLK - jnp.floor_divide(key_index, BLK)
    entries = jnp.arange(slash_offsets.shape[1])
    slash_live = entries[None, :] < slash_count[:, None]
    matched = jnp.any(
        (slash_offsets[:, :, None, None] == block_gap[None, None]) & slash_live[:, :, None, None],
        axis=1,
    )
    diagonal = (block_gap == 0) & (key_index <= row_index)
    present = seq_index * tok_rows + key_index >= 0
    allowed = (matched | diagonal[None]) & present[None]
    scores = jnp.where(allowed[:, None], scores, -jnp.inf)
    running_max = jnp.max(scores, axis=-1)
    weights = jnp.exp(scores - running_max[..., None])
    running_sum = jnp.sum(weights, axis=-1)
    accumulate = jnp.einsum(
        "kgtn,nkh->kgth",
        weights.astype(jnp.bfloat16),
        near_values,
        preferred_element_type=jnp.float32,
    )
    carried = (
        running_max.reshape(local_heads, -1),
        running_sum.reshape(local_heads, -1),
        accumulate.reshape(local_heads, -1, head_dim),
    )
    per_device = cache_keys.shape[1] // BLK
    first_block = seq_index * per_device
    cache_pairs = jnp.stack([cache_keys, cache_values], 1).reshape(
        local_heads, 2, per_device, BLK, head_dim
    )
    entry_index = jnp.arange(vert_blocks.shape[1])
    owned_here = (
        (entry_index[None, :] < vert_count[:, None])
        & (vert_blocks >= first_block)
        & (vert_blocks < first_block + per_device)
    )
    rank_slot = jnp.cumsum(owned_here.astype(jnp.int32), axis=1) - 1
    selector = (rank_slot[:, None, :] == jnp.arange(VCAP)[None, :, None]) & owned_here[:, None, :]
    slot_ids = jnp.sum(jnp.where(selector, vert_blocks[:, None, :], 0), axis=2)
    slot_live = jnp.any(selector, axis=2)
    local_index = jnp.clip(slot_ids - first_block, 0, per_device - 1)
    taken_rows = jnp.take_along_axis(cache_pairs, local_index[:, None, :, None, None], axis=2)
    taken_rows = jnp.where(
        slot_live[:, None, :, None, None], taken_rows, jnp.zeros((), taken_rows.dtype)
    )
    kv_slots = taken_rows.transpose(2, 0, 1, 3, 4)
    carried = attend_slots(
        carried,
        lax.all_gather(kv_slots, "seq", axis=0, tiled=True),
        lax.all_gather(slot_live.T.astype(jnp.int32), "seq", axis=0, tiled=True) > 0,
        head_queries,
        score_scale,
    )
    running_max, running_sum, accumulate = carried
    attended = (accumulate / running_sum[..., None]).reshape(
        local_heads, group_size, tok_rows, head_dim
    )
    attended = (
        attended.transpose(2, 0, 1, 3)
        .reshape(tok_rows, local_heads * group_size * head_dim)
        .astype(jnp.bfloat16)
    )
    summed = lax.psum_scatter(
        lax.dot_general(
            w_out, attended, (((0,), (1,)), ((), ())), preferred_element_type=jnp.float32
        ).astype(jnp.bfloat16),
        "heads",
        scatter_dimension=0,
        tiled=True,
    ).astype(jnp.float32)
    return summed.T.astype(jnp.bfloat16)


def solution(mesh):
    return jax.shard_map(
        local,
        mesh=mesh,
        in_specs=(
            P("seq", None),
            P(),
            P(None, "heads"),
            P(None, "heads"),
            P(None, "heads"),
            P("heads", None),
            P("heads", "seq", None),
            P("heads", "seq", None),
            P("heads", None),
            P("heads"),
            P("heads", None),
            P("heads"),
        ),
        out_specs=P("seq", "heads"),
        check_vma=False,
    )
```

profile of v0, /device:TPU:6, one launch (start us, length us, event | category | flops | bytes accessed | tf_op | source)
XLA Modules:
  0.0 209.7 jit_solution(15901968722677744452)
XLA Ops:
  7.3 0.8 convert_bitcast_fusion
  9.4 1.9 maximum_bitcast_fusion
  11.3 1.6 gather_fusion
  13.8 2.2 %fusion.18 = f32[256]{0:T(256)S(1)} fusion(bf16[256,4096]{1,0:T(8,128)(2,1)} %param.14), kind=kLoop, calls=%fused_computation.26 | loop fusion | flops 3145472 | bytes 2098176 | tf_op jit(solution)/shard_map/reduce_sum | solution.py:82
  16.1 1.4 convolution_convert_fusion.2
  17.5 4.4 %collective-permute-start.1 = (bf16[256,128]{1,0:T(8,128)(2,1)}, bf16[256,128]{1,0:T(8,128)(2,1)}, u32[]{:S(2)}, u32[]{:S(2)}) collective-permute-start(bf16[256,128]{1,0:T(8,128)(2,1)} %convolution_convert_fusion.2), channel_id=1, source_target_pairs={{0,1},{1,2},{2,3},{3,4},{4,5},{5,6},{6,7},{7,8},{8,9},{9,10},{10,1... | collective-permute-start | bytes 196616 | tf_op jit(solution)/shard_map/ppermute | solution.py:15
  21.9 1.4 convolution_convert_fusion.3
  23.4 3.8 %collective-permute-start = (bf16[256,128]{1,0:T(8,128)(2,1)}, bf16[256,128]{1,0:T(8,128)(2,1)}, u32[]{:S(2)}, u32[]{:S(2)}) collective-permute-start(bf16[256,128]{1,0:T(8,128)(2,1)} %convolution_convert_fusion.3), channel_id=1, source_target_pairs={{0,1},{1,2},{2,3},{3,4},{4,5},{5,6},{6,7},{7,8},{8,9},{9,10},{10,1... | collective-permute-start | bytes 196616 | tf_op jit(solution)/shard_map/ppermute | solution.py:15
  29.2 20.6 %all-reduce = s32[256]{0:T(256)S(1)} all-reduce(s32[256]{0:T(256)S(1)} %convert_dynamic-update-slice_fusion), channel_id=2, replica_groups=mesh['heads'=8,'seq'=32] {'seq'}, use_global_device_ids=true, to_apply=%add | all-reduce | flops 256 | bytes 2048
  50.6 3.5 %convolution_convert_fusion.1 = bf16[256,512]{1,0:T(8,128)(2,1)S(1)} fusion(bf16[4096,512]{1,0:T(8,128)(2,1)} %param.16, bf16[256,4096]{1,0:T(8,128)(2,1)S(1)} %copy-done.1, f32[4096]{0:T(1024)} %param.15, f32[256]{0:T(256)S(1)} %add_rsqrt_fusion), kind=kOutput, calls=%fused_computation.35 | convolution fusion | flops 1078067200 | bytes 6571008 | tf_op jit(solution)/shard_map/dot_general | solution.py:85
  55.4 1.4 fusion.47
  57.1 1.4 convolution_bitcast_fusion
  58.5 56.5 %all-gather.3.cloned.1.call-done = bf16[256,1,2,64,128]{4,3,2,1,0:T(8,128)(2,1)} async-done(((bf16[8,1,2,64,128]{4,3,2,1,0:T(8,128)(2,1)}), bf16[256,1,2,64,128]{4,3,2,1,0:T(8,128)(2,1)}) %all-gather.3.cloned.1.call-update) | async-done | bytes 8388624 | tf_op jit(solution)/shard_map/all_gather | solution.py:156
  115.0 52.6 %while.14 = (s32[]{:T(128)}, f32[1,1024]{1,0:T(1,128)S(1)}, f32[1,1024]{1,0:T(1,128)S(1)}, f32[1,1024,128]{2,1,0:T(8,128)S(1)}, pred[8,32,1]{1,2,0:T(4,128)(4,1)...) while((s32[]{:T(128)}, f32[1,1024]{1,0:T(1,128)S(1)}, ...), condition=%wide.region_10.11_spmd, body=%wide.region_7.10_spmd.sunk | while | flops 1097074688 | bytes 29689028 | solution.py:55
  115.0 1.3 copy_bitcast_fusion.2
  116.3 1.3 fusion.59
  117.6 1.9 fusion.60
  119.5 2.1 fusion.61
  121.6 1.3 copy_bitcast_fusion.2
  122.9 1.3 fusion.59
  124.2 1.9 fusion.60
  126.1 2.1 fusion.61
  128.2 1.3 copy_bitcast_fusion.2
  129.5 1.3 fusion.59
  130.7 1.9 fusion.60
  132.6 2.1 fusion.61
  134.7 1.3 copy_bitcast_fusion.2
  136.0 1.3 fusion.59
  137.3 1.9 fusion.60
  139.2 2.1 fusion.61
  141.3 1.3 copy_bitcast_fusion.2
  142.6 1.3 fusion.59
  143.9 1.9 fusion.60
  145.8 2.1 fusion.61
  147.9 1.3 copy_bitcast_fusion.2
  149.2 1.3 fusion.59
  150.5 1.9 fusion.60
  152.4 2.1 fusion.61
  154.5 1.3 copy_bitcast_fusion.2
  155.8 1.3 fusion.59
  157.1 1.9 fusion.60
  158.9 2.1 fusion.61
  161.1 1.3 copy_bitcast_fusion.2
  162.4 1.3 fusion.59
  163.6 1.9 fusion.60
  165.5 2.1 fusion.61
  168.0 4.8 %fusion.17 = bf16[4096,256]{0,1:T(8,128)(2,1)} fusion(bf16[256,512]{0,1:T(8,128)(2,1)S(1)} %bitcast.119, bf16[512,4096]{1,0:T(8,128)(2,1)} %param.19), kind=kOutput, calls=%fused_computation.25 | convolution fusion | flops 1074790400 | bytes 6553600 | tf_op jit(solution)/shard_map/dot_general | solution.py:171
  172.8 30.0 %reduce-scatter.2.cloned.1.call-done = bf16[512,256]{0,1:T(8,128)(2,1)} async-done(((bf16[4096,256]{0,1:T(8,128)(2,1)}), bf16[512,256]{0,1:T(8,128)(2,1)}) %reduce-scatter.2.cloned.1.call-update) | async-done | bytes 262160 | tf_op jit(solution)/shard_map/reduce_scatter | solution.py:170
  (80 shorter events, 5.8 us)
Async XLA Ops:
  6.5 9.5 %copy-start = (bf16[4096,128]{1,0:T(8,128)(2,1)S(1)}, bf16[4096,128]{1,0:T(8,128)(2,1)}, u32[]{:S(2)}) copy-start(bf16[4096,128]{1,0:T(8,128)(2,1)} %param.18) | copy-start | bytes 3145732
  6.5 9.5 %copy-start.1 = (bf16[256,4096]{1,0:T(8,128)(2,1)S(1)}, bf16[256,4096]{1,0:T(8,128)(2,1)}, u32[]{:S(2)}) copy-start(bf16[256,4096]{1,0:T(8,128)(2,1)} %param.14) | copy-start | bytes 6291460
  6.5 9.5 %copy-start.4 = (f32[4096]{0:T(1024)S(1)}, f32[4096]{0:T(1024)}, u32[]{:S(2)}) copy-start(f32[4096]{0:T(1024)} %param.15) | copy-start | bytes 49156
  6.5 108.5 %all-gather.3.cloned.1.call-start = ((), (), s32[]{:S(2)}) async-start(), calls=%async_computation.1 | async-start | bytes 8650752 | tf_op jit(solution)/shard_map/all_gather | solution.py:156
  13.8 189.1 %reduce-scatter.2.cloned.1.call-start = ((), (), s32[]{:S(2)}) async-start(), calls=%async_computation.2 | async-start | bytes 2359296 | tf_op jit(solution)/shard_map/reduce_scatter | solution.py:170
  13.8 8.1 %copy-start.3 = (bf16[4096,128]{1,0:T(8,128)(2,1)S(1)}, bf16[4096,128]{1,0:T(8,128)(2,1)}, u32[]{:S(2)}) copy-start(bf16[4096,128]{1,0:T(8,128)(2,1)} %param.17) | copy-start | bytes 3145732
  16.0 11.8 %copy-start.5 = (u32[256]{0:T(256)S(1)}, u32[256]{0:T(256)}, u32[]{:S(2)}) copy-start(u32[256]{0:T(256)} %constant.100) | copy-start | bytes 3076
  16.1 33.9 %copy-start.2 = (s32[1,4]{1,0:T(1,128)S(1)}, s32[1,4]{1,0:T(1,128)}, u32[]{:S(2)}) copy-start(s32[1,4]{1,0:T(1,128)} %param.24) | copy-start | bytes 52
  17.5 39.6 %collective-permute-start.1 = (bf16[256,128]{1,0:T(8,128)(2,1)}, bf16[256,128]{1,0:T(8,128)(2,1)}, u32[]{:S(2)}, u32[]{:S(2)}) collective-permute-start(bf16[256,128]{1,0:T(8,128)(2,1)} %convolution_convert_fusion.2), channel_id=1, source_target_pairs={{0,1},{1,2},{2,3},{3,4},{4,5},{5,6},{6,7},{7,8},{8,9},{9,10},{10,1... | collective-permute-start | bytes 196616 | tf_op jit(solution)/shard_map/ppermute | solution.py:15
  23.4 32.0 %collective-permute-start = (bf16[256,128]{1,0:T(8,128)(2,1)}, bf16[256,128]{1,0:T(8,128)(2,1)}, u32[]{:S(2)}, u32[]{:S(2)}) collective-permute-start(bf16[256,128]{1,0:T(8,128)(2,1)} %convolution_convert_fusion.3), channel_id=1, source_target_pairs={{0,1},{1,2},{2,3},{3,4},{4,5},{5,6},{6,7},{7,8},{8,9},{9,10},{10,1... | collective-permute-start | bytes 196616 | tf_op jit(solution)/shard_map/ppermute | solution.py:15
Sparse Core Ops, SparseCore 0:
  13.9 101.0 all-gather.2
  172.9 29.8 reduce-scatter.1
where the time goes:
time: 214 us; the launch traced here: 210 us
  waiting for transfers between devices  86.6 us (40%)
  matrix products  40.5 us (19%)
  other arithmetic  23.3 us (11%)
  blocking collectives  20.6 us (10%)
  between operations  15.7 us (7%)
  local copies, waits for them, and re-layouts  14.2 us (7%)
  starting transfers between devices  8.3 us (4%)
    all_gather x1, waiting for transfers between devices, local(): lax.all_gather(kv_slots, 'seq', axis=0, tiled=True)  56.5 us
    reduce_scatter x1, waiting for transfers between devices, local(): lax.psum_scatter(lax.dot_general(w_out, attended, (((0,), (1,)), ((), ())...  30 us
    unnamed x1, blocking collectives  20.6 us
    dot_general x8, matrix products, fold_step(): jnp.einsum('krsn,sknh->krh', rounded, kv_block[:, :, 1], preferred_elemen...  16.5 us
    reduce_sum x8, other arithmetic, fold_step(): running_sum = running_sum * factor + jnp.sum(weights, axis=-1)  14.9 us
    squeeze x8, local copies, waits for them, and re-layouts, attend_slots(): result, _ = lax.scan(fold_step, carried, (stacked, grouped_flags))  10.4 us
    dot_general x8, matrix products, fold_step(): jnp.einsum('krh,sknh->krsn', head_queries, kv_block[:, :, 0], preferred_e...  10.1 us
    ppermute x2, starting transfers between devices, passed_along(): return lax.ppermute(block, axis, route)  8.26 us
  transfers between devices with their start and end apart: 4, of which 2 were waited for; matrix products, arithmetic and copies ran while one was open for 7% of the time, Pallas kernels for 0%

commit v1 on v0

v1 whole, which is shorter than its diff:
```python
import functools
import math

import jax
import jax.numpy as jnp
from jax import lax
from jax.experimental import pallas as pl
from jax.experimental.pallas import tpu as pltpu
from jax.sharding import PartitionSpec as P

BLK = 64
HD = 128
GROUP = 4
NY = 4
NZ = 8
NX = 4
VMEM = pltpu.VMEM
VSPEC = pl.BlockSpec(memory_space=pltpu.VMEM)
SSPEC = pl.BlockSpec(memory_space=pltpu.SMEM)
SCALE2 = math.log2(math.e) / math.sqrt(HD)
NEG = -jnp.inf


def params(mib):
    return pltpu.CompilerParams(vmem_limit_bytes=mib << 20)


def shift_y(block, d):
    return lax.ppermute(
        block, "seq", [(y * NZ + z, (y + d) % NY * NZ + z) for y in range(NY) for z in range(NZ)]
    )


def shift_z(block, d):
    return lax.ppermute(
        block, "seq", [(y * NZ + z, y * NZ + (z + d) % NZ) for y in range(NY) for z in range(NZ)]
    )


def shift_x(block, d):
    return lax.ppermute(
        block, "heads", [(2 * x + c, 2 * ((x + d) % NX) + c) for x in range(NX) for c in range(2)]
    )


def swap_core(block):
    return lax.ppermute(block, "heads", [(i, i ^ 1) for i in range(2 * NX)])


def position():
    me = lax.axis_index("seq")
    return me // NZ, lax.rem(me, NZ)


def pick_kernel(tab, cs, ck, cv, *outs):
    y, z = position()
    group = z * NY + y
    start = cs[group]
    size = cs[group + 1] - start
    for dy in range(NY):
        for j in range(2):
            i = ((y + dy - start) & 3) + 4 * j
            entry = tab[jnp.minimum(start + i, 63)]
            row = pl.multiple_of(jnp.where(i < size, entry & 15, 0) * BLK, BLK)
            outs[dy][j, 0] = ck[0, pl.ds(row, BLK), :]
            outs[dy][j, 1] = cv[0, pl.ds(row, BLK), :]


def column_kernel(tab, cs, r0, r1, r2, r3, out):
    y, z = position()
    recv = (r0, r1, r2, r3)
    start = cs[z * NY]
    size = cs[z * NY + NY] - start
    first = (y - start) & 3
    for i in range(8):
        off = first + 4 * i
        live = off < size
        r = jnp.minimum(start + off, 63)
        entry = tab[r]
        hy = (entry >> 4) & 3
        j = jnp.where(live, (r - cs[z * NY + hy]) >> 2, 0)
        d = jnp.where(live, (y - hy) & 3, 0)
        for k in range(NY):

            @pl.when(d == k)
            def _():
                out[i] = recv[k][j]


def row_kernel(tab, cs, count, *refs):
    y, z = position()
    recv, out = refs[:NZ], refs[NZ]
    for m in range(16):
        r = y + 4 * m
        live = r < count[0]
        entry = tab[r]
        zs = jnp.where(live, entry >> 6, z)
        start = cs[zs * NY]
        first = (y - start) & 3
        i = jnp.where(live, (r - start - first) >> 2, 0)
        d = (z - zs) & 7
        for k in range(NZ):

            @pl.when(d == k)
            def _():
                out[0, m * BLK : (m + 1) * BLK] = recv[k][i, 0]
                out[1, m * BLK : (m + 1) * BLK] = recv[k][i, 1]


def near_kernel(offs, cnt, q, kp, vp, k, v, m_out, l_out, acc_out):
    me = lax.axis_index("seq")
    rows = k.shape[0]
    keys = jnp.concatenate([kp[...], k[...]], axis=0)
    values = jnp.concatenate([vp[...], v[...]], axis=0)
    t = lax.broadcasted_iota(jnp.int32, (rows, 2 * rows), 0)
    u = lax.broadcasted_iota(jnp.int32, (rows, 2 * rows), 1) - rows
    gap = (t >> 6) - (u >> 6)
    hit = (gap == 0) & (u <= t)
    for e in range(4):
        off = jnp.where((e < cnt[0]) & (offs[0, e] >= 0), offs[0, e], -100)
        hit = hit | (gap == off)
    hit = hit & (u >= jnp.where(me > 0, -rows, 0))
    for h in range(GROUP):
        s = lax.dot_general(
            q[:, h * HD : (h + 1) * HD],
            keys,
            (((1,), (1,)), ((), ())),
            preferred_element_type=jnp.float32,
        )
        s = jnp.where(hit, s, NEG)
        top = jnp.max(s, axis=1, keepdims=True)
        p = jnp.exp2((s - top) * SCALE2)
        m_out[h] = jnp.broadcast_to(top, (rows, HD))
        l_out[h] = jnp.broadcast_to(jnp.sum(p, axis=1, keepdims=True), (rows, HD))
        acc_out[h] = jnp.dot(p.astype(jnp.bfloat16), values, preferred_element_type=jnp.float32)


def far_step(count, shift, q, kv, m_in, l_in, acc_in, h):
    y, _ = position()
    src = (y - shift) & 3
    live = ((count[0] - src + 3) >> 2) * BLK
    s = lax.dot_general(
        q[:, h * HD : (h + 1) * HD],
        kv[0],
        (((1,), (1,)), ((), ())),
        preferred_element_type=jnp.float32,
    )
    key = lax.broadcasted_iota(jnp.int32, s.shape, 1)
    s = jnp.where(key < live, s, NEG)
    old = m_in[h][:, :1]
    top = jnp.maximum(old, jnp.max(s, axis=1, keepdims=True))
    factor = jnp.exp2((old - top) * SCALE2)
    p = jnp.exp2((s - top) * SCALE2)
    total = l_in[h][:, :1] * factor + jnp.sum(p, axis=1, keepdims=True)
    acc = acc_in[h] * factor + jnp.dot(
        p.astype(jnp.bfloat16), kv[1], preferred_element_type=jnp.float32
    )
    return top, total, acc


def far_kernel(shift, count, q, kv, m_in, l_in, acc_in, m_out, l_out, acc_out):
    for h in range(GROUP):
        top, total, acc = far_step(count, shift, q, kv, m_in, l_in, acc_in, h)
        m_out[h] = jnp.broadcast_to(top, m_out.shape[1:])
        l_out[h] = jnp.broadcast_to(total, l_out.shape[1:])
        acc_out[h] = acc


def last_kernel(shift, count, q, kv, m_in, l_in, acc_in, att):
    for h in range(GROUP):
        _, total, acc = far_step(count, shift, q, kv, m_in, l_in, acc_in, h)
        att[:, h * HD : (h + 1) * HD] = (acc / total).astype(jnp.bfloat16)


def away_kernel(cols, att, w, out):
    out[0] = jnp.dot(att[...], w[...], preferred_element_type=jnp.float32).astype(out.dtype)


def home_kernel(cols, att, w, recv, out):
    mine = jnp.dot(att[...], w[...], preferred_element_type=jnp.float32)
    out[...] = (mine + recv[0].astype(jnp.float32)).astype(out.dtype)


def final_kernel(mine, a, b, c, out):
    total = mine[...] + a[...].astype(jnp.float32)
    total = total + b[...].astype(jnp.float32) + c[...].astype(jnp.float32)
    out[...] = total.astype(out.dtype)


def local(
    tokens,
    norm_gain,
    w_query,
    w_key,
    w_value,
    w_out,
    cache_keys,
    cache_values,
    vert_blocks,
    vert_count,
    slash_offsets,
    slash_count,
):
    rows = tokens.shape[0]
    bf16 = jnp.bfloat16
    f32 = jnp.float32
    blocks = vert_blocks[0]
    entry = jnp.arange(64, dtype=jnp.int32)
    key = jnp.where(
        entry < vert_count[0],
        (((blocks >> 4) & 7) << 6) | ((blocks >> 7) << 4) | (blocks & 15),
        4096 + entry,
    )
    edges = jnp.concatenate([key, jnp.arange(64, dtype=jnp.int32) * 16])
    below = jnp.sum((key[None, :] < edges[:, None]).astype(jnp.int32), axis=1)
    rank, cs = below[:64], below[64:]
    tab = jnp.sum(jnp.where(rank[None, :] == entry[:, None], key[None, :], 0), axis=1)

    slot = jax.ShapeDtypeStruct((2, 2, BLK, HD), bf16)
    picked = pl.pallas_call(
        pick_kernel,
        out_shape=[slot] * NY,
        in_specs=[SSPEC, SSPEC, VSPEC, VSPEC],
        out_specs=[VSPEC] * NY,
        compiler_params=params(8),
        name="pick",
    )(tab, cs, cache_keys, cache_values)
    spread = [picked[0]] + [shift_y(picked[d], d) for d in range(1, NY)]
    column = pl.pallas_call(
        column_kernel,
        out_shape=jax.ShapeDtypeStruct((8, 2, BLK, HD), bf16),
        in_specs=[SSPEC, SSPEC] + [VSPEC] * NY,
        out_specs=VSPEC,
        compiler_params=params(8),
        name="column",
    )(tab, cs, *spread)
    ring = [column] + [None] * 7
    ring[1], ring[7] = shift_z(column, 1), shift_z(column, -1)
    ring[2], ring[6] = shift_z(ring[1], 1), shift_z(ring[7], -1)
    ring[3], ring[5] = shift_z(ring[2], 1), shift_z(ring[6], -1)
    ring[4] = shift_z(ring[3], 1)
    own = pl.pallas_call(
        row_kernel,
        out_shape=jax.ShapeDtypeStruct((2, 16 * BLK, HD), bf16),
        in_specs=[SSPEC] * 3 + [VSPEC] * NZ,
        out_specs=VSPEC,
        compiler_params=params(16),
        name="row",
    )(tab, cs, vert_count, *ring)
    parts = [own] + [shift_y(own, d) for d in (1, 3, 2)]

    activation = tokens.astype(f32)
    normed = (
        activation
        * lax.rsqrt(jnp.mean(activation * activation, axis=-1, keepdims=True) + 1e-05)
        * norm_gain
    ).astype(bf16)
    key_rows = jnp.dot(normed, w_key, preferred_element_type=f32).astype(bf16)
    value_rows = jnp.dot(normed, w_value, preferred_element_type=f32).astype(bf16)
    seqs = lax.axis_size("seq")
    route = [(i, (i + 1) % seqs) for i in range(seqs)]
    before_keys, before_values = lax.ppermute((key_rows, value_rows), "seq", route)
    queries = jnp.dot(normed, w_query, preferred_element_type=f32).astype(bf16)

    state_shape = [jax.ShapeDtypeStruct((GROUP, rows, HD), f32)] * 3
    state = pl.pallas_call(
        near_kernel,
        out_shape=state_shape,
        in_specs=[SSPEC] * 2 + [VSPEC] * 5,
        out_specs=[VSPEC] * 3,
        compiler_params=params(24),
        name="near",
    )(slash_offsets, slash_count, queries, before_keys, before_values, key_rows, value_rows)
    for shift, part in zip((0, 1, 3), parts):
        state = pl.pallas_call(
            functools.partial(far_kernel, shift),
            out_shape=state_shape,
            in_specs=[SSPEC] + [VSPEC] * 5,
            out_specs=[VSPEC] * 3,
            compiler_params=params(24),
            name="far",
        )(vert_count, queries, part, *state)
    attended = pl.pallas_call(
        functools.partial(last_kernel, 2),
        out_shape=jax.ShapeDtypeStruct((rows, GROUP * HD), bf16),
        in_specs=[SSPEC] + [VSPEC] * 5,
        out_specs=VSPEC,
        compiler_params=params(24),
        name="last",
    )(vert_count, queries, parts[3], *state)

    heads = lax.axis_index("heads")
    x, core = heads // 2, lax.rem(heads, 2)
    depth = GROUP * HD
    order = (x + jnp.arange(NX, dtype=jnp.int32)) & 3
    away = pl.pallas_call(
        away_kernel,
        out_shape=jax.ShapeDtypeStruct((NX, rows, depth), bf16),
        grid_spec=pltpu.PrefetchScalarGridSpec(
            num_scalar_prefetch=1,
            grid=(NX,),
            in_specs=[
                pl.BlockSpec((rows, depth), lambda i, cols: (0, 0)),
                pl.BlockSpec((depth, depth), lambda i, cols: (0, cols[i])),
            ],
            out_specs=pl.BlockSpec((1, rows, depth), lambda i, cols: (i, 0, 0)),
        ),
        compiler_params=params(16),
        name="away",
    )(order * 2 + 1 - core, attended, w_out)
    recv = swap_core(away)
    home_cols = order * 2 + core

    def home(d, dtype):
        return pl.pallas_call(
            home_kernel,
            out_shape=jax.ShapeDtypeStruct((rows, depth), dtype),
            grid_spec=pltpu.PrefetchScalarGridSpec(
                num_scalar_prefetch=1,
                grid=(1,),
                in_specs=[
                    pl.BlockSpec((rows, depth), lambda i, cols: (0, 0)),
                    pl.BlockSpec((depth, depth), lambda i, cols: (0, cols[d])),
                    pl.BlockSpec((1, rows, depth), lambda i, cols: (d, 0, 0)),
                ],
                out_specs=pl.BlockSpec((rows, depth), lambda i, cols: (0, 0)),
            ),
            compiler_params=params(16),
            name="home",
        )(home_cols, attended, w_out, recv)

    sums = [shift_x(home(d, bf16), d) for d in (2, 1, 3)]
    return pl.pallas_call(
        final_kernel,
        out_shape=jax.ShapeDtypeStruct((rows, depth), bf16),
        in_specs=[VSPEC] * 4,
        out_specs=VSPEC,
        compiler_params=params(16),
        name="final",
    )(home(0, f32), *sums)


def solution(mesh):
    return jax.shard_map(
        local,
        mesh=mesh,
        in_specs=(
            P("seq", None),
            P(),
            P(None, "heads"),
            P(None, "heads"),
            P(None, "heads"),
            P("heads", None),
            P("heads", "seq", None),
            P("heads", "seq", None),
            P("heads", None),
            P("heads"),
            P("heads", None),
            P("heads"),
        ),
        out_specs=P("seq", "heads"),
        check_vma=False,
    )
```

time: 214 us -> 102 us (0.48)
  the two profiles are of different devices: /device:TPU:6 before, /device:TPU:24 now
where the time goes in v1:
time: 102 us
  waiting for transfers between devices  41.9 us (41%)
  starting transfers between devices  24.3 us (24%)
  Pallas kernels  21.2 us (21%)
  matrix products  7.38 us (7%)
  other arithmetic  3.06 us (3%)
  local copies, waits for them, and re-layouts  2 us (2%)
  between operations  1.66 us (2%)
    ppermute x7, waiting for transfers between devices, shift_z(): lax.ppermute(block, 'seq', [(y * NZ + z, y * NZ + (z + d) % NZ) for y in...  14.7 us
    ppermute x6, waiting for transfers between devices, shift_y(): lax.ppermute(block, 'seq', [(y * NZ + z, (y + d) % NY * NZ + z) for y in...  13.7 us
    ppermute x7, starting transfers between devices, shift_z(): lax.ppermute(block, 'seq', [(y * NZ + z, y * NZ + (z + d) % NZ) for y in...  12.7 us
    ppermute x3, waiting for transfers between devices, shift_x(): lax.ppermute(block, 'heads', [(2 * x + c, 2 * ((x + d) % NX) + c) for x i...  10.8 us
    pallas_call x3, Pallas kernels, local(): pl.pallas_call(functools.partial(far_kernel, shift), out_shape=state_shap...  7.57 us
    ppermute x6, starting transfers between devices, shift_y(): lax.ppermute(block, 'seq', [(y * NZ + z, (y + d) % NY * NZ + z) for y in...  5.53 us
    ppermute x3, starting transfers between devices, shift_x(): lax.ppermute(block, 'heads', [(2 * x + c, 2 * ((x + d) % NX) + c) for x i...  5.25 us
    dot_general x1, matrix products, local(): queries = jnp.dot(normed, w_query, preferred_element_type=f32).astype(bf16)  4.12 us
  transfers between devices with their start and end apart: 19, of which 12 were waited for; matrix products, arithmetic and copies ran while one was open for 9% of the time, Pallas kernels for 13%

profile of v1, /device:TPU:24, one launch (start us, length us, event | category | flops | bytes accessed | tf_op | source)
XLA Modules:
  0.0 101.6 jit_solution(12445927970990815630)
XLA Ops:
  0.7 0.7 compare_select_fusion
  1.7 0.1 select_reduce_fusion.tab
  1.8 0.9 copy-done.2
  2.7 0.9 copy-done.3
  3.7 0.6 pick.1
  4.3 2.0 %collective-permute-start = (bf16[2,2,64,128]{3,2,1,0:T(8,128)(2,1)S(1)}, bf16[2,2,64,128]{3,2,1,0:T(8,128)(2,1)S(1)}, u32[]{:S(2)}, u32[]{:S(2)}) collective-permute-start(bf16[2,2,64,128]{3,2,1,0:T(8,128)(2,1)S(1)} %get-tuple-element.22), channel_id=1, source_target_pairs={{0,8},{1,9},{2,10},{3,11},{4,12},{5,13},{6,14},{7,15},{8,16},{9,17... | collective-permute-start | bytes 196616 | tf_op jit(solution)/shard_map/ppermute | solution.py:29
  6.3 0.9 collective-permute-start.1
  7.2 0.1 collective-permute-start.2
  7.3 1.6 %collective-permute-done.r1 = bf16[2,2,64,128]{3,2,1,0:T(8,128)(2,1)S(1)} collective-permute-done((bf16[2,2,64,128]{3,2,1,0:T(8,128)(2,1)S(1)}, bf16[2,2,64,128]{3,2,1,0:T(8,128)(2,1)S(1)}, u32[]{:S(2)}, u32[]{:S(2)}) %collective-permute-start) | collective-permute-done | bytes 65568 | tf_op jit(solution)/shard_map/ppermute | solution.py:29
  8.9 3.2 %collective-permute-done.1.r2 = bf16[2,2,64,128]{3,2,1,0:T(8,128)(2,1)S(1)} collective-permute-done((bf16[2,2,64,128]{3,2,1,0:T(8,128)(2,1)S(1)}, bf16[2,2,64,128]{3,2,1,0:T(8,128)(2,1)S(1)}, u32[]{:S(2)}, u32[]{:S(2)}) %collective-permute-start.1) | collective-permute-done | bytes 65568 | tf_op jit(solution)/shard_map/ppermute | solution.py:29
  12.1 0.7 collective-permute-done.2.r3
  12.8 0.8 column.1.refs_0_
  13.6 1.9 %collective-permute-start.3 = (bf16[8,2,64,128]{3,2,1,0:T(8,128)(2,1)S(1)}, bf16[8,2,64,128]{3,2,1,0:T(8,128)(2,1)S(1)}, u32[]{:S(2)}, u32[]{:S(2)}) collective-permute-start(bf16[8,2,64,128]{3,2,1,0:T(8,128)(2,1)S(1)} %column.1.refs_0_), channel_id=1, source_target_pairs={{0,1},{1,2},{2,3},{3,4},{4,5},{5,6},{6,7},{7,0},{8,9},{9,10},{10,1... | collective-permute-start | bytes 786440 | tf_op jit(solution)/shard_map/ppermute | solution.py:35
  15.5 4.0 %collective-permute-start.7 = (bf16[8,2,64,128]{3,2,1,0:T(8,128)(2,1)S(1)}, bf16[8,2,64,128]{3,2,1,0:T(8,128)(2,1)S(1)}, u32[]{:S(2)}, u32[]{:S(2)}) collective-permute-start(bf16[8,2,64,128]{3,2,1,0:T(8,128)(2,1)S(1)} %column.1.refs_0_), channel_id=1, source_target_pairs={{0,7},{1,0},{2,1},{3,2},{4,3},{5,4},{6,5},{7,6},{8,15},{9,8},{10,9... | collective-permute-start | bytes 786440 | tf_op jit(solution)/shard_map/ppermute | solution.py:35
  19.5 4.6 %collective-permute-done.3.refs_1_ = bf16[8,2,64,128]{3,2,1,0:T(8,128)(2,1)S(1)} collective-permute-done((bf16[8,2,64,128]{3,2,1,0:T(8,128)(2,1)S(1)}, bf16[8,2,64,128]{3,2,1,0:T(8,128)(2,1)S(1)}, u32[]{:S(2)}, u32[]{:S(2)}) %collective-permute-start.3) | collective-permute-done | bytes 262176 | tf_op jit(solution)/shard_map/ppermute | solution.py:35
  24.1 2.1 %fusion = f32[256]{0:T(256)S(1)} fusion(bf16[256,4096]{1,0:T(8,128)(2,1)} %param.12), kind=kLoop, calls=%fused_computation.2 | loop fusion | flops 3145472 | bytes 2098176 | tf_op jit(solution)/shard_map/reduce_sum | solution.py:255
  26.2 3.3 %collective-permute-start.8 = (bf16[8,2,64,128]{3,2,1,0:T(8,128)(2,1)S(1)}, bf16[8,2,64,128]{3,2,1,0:T(8,128)(2,1)S(1)}, u32[]{:S(2)}, u32[]{:S(2)}) collective-permute-start(bf16[8,2,64,128]{3,2,1,0:T(8,128)(2,1)S(1)} %collective-permute-done.7.refs_7_), channel_id=1, source_target_pairs={{0,7},{1,0},{2,1},{3,2},{4,3},{5,4},{6,5},{7,6},{8,15},{9,8},{10,9... | collective-permute-start | bytes 786440 | tf_op jit(solution)/shard_map/ppermute | solution.py:35
  29.5 2.2 %collective-permute-done.4.refs_2_ = bf16[8,2,64,128]{3,2,1,0:T(8,128)(2,1)S(1)} collective-permute-done((bf16[8,2,64,128]{3,2,1,0:T(8,128)(2,1)S(1)}, bf16[8,2,64,128]{3,2,1,0:T(8,128)(2,1)S(1)}, u32[]{:S(2)}, u32[]{:S(2)}) %collective-permute-start.4) | collective-permute-done | bytes 262176 | tf_op jit(solution)/shard_map/ppermute | solution.py:35
  31.7 2.4 %convolution_convert_fusion.2.k = bf16[256,128]{1,0:T(8,128)(2,1)S(1)} fusion(bf16[4096,128]{1,0:T(8,128)(2,1)S(1)} %copy-done, bf16[256,4096]{1,0:T(8,128)(2,1)} %param.12, f32[4096]{0:T(1024)} %param.13, f32[256]{0:T(256)S(1)} %add_rsqrt_fusion), kind=kOutput, calls=%fused_computation.7 | convolution fusion | flops 272662528 | bytes 3228672 | tf_op jit(solution)/shard_map/dot_general | solution.py:258
  34.2 3.5 %collective-permute-start.9 = (bf16[8,2,64,128]{3,2,1,0:T(8,128)(2,1)S(1)}, bf16[8,2,64,128]{3,2,1,0:T(8,128)(2,1)S(1)}, u32[]{:S(2)}, u32[]{:S(2)}) collective-permute-start(bf16[8,2,64,128]{3,2,1,0:T(8,128)(2,1)S(1)} %collective-permute-done.8.refs_6_), channel_id=1, source_target_pairs={{0,7},{1,0},{2,1},{3,2},{4,3},{5,4},{6,5},{7,6},{8,15},{9,8},{10,9... | collective-permute-start | bytes 786440 | tf_op jit(solution)/shard_map/ppermute | solution.py:35
  37.7 2.4 %collective-permute-done.5.refs_3_ = bf16[8,2,64,128]{3,2,1,0:T(8,128)(2,1)S(1)} collective-permute-done((bf16[8,2,64,128]{3,2,1,0:T(8,128)(2,1)S(1)}, bf16[8,2,64,128]{3,2,1,0:T(8,128)(2,1)S(1)}, u32[]{:S(2)}, u32[]{:S(2)}) %collective-permute-start.5) | collective-permute-done | bytes 262176 | tf_op jit(solution)/shard_map/ppermute | solution.py:35
  40.1 0.9 convolution_convert_fusion.1.v
  41.0 0.5 collective-permute-start.14
  42.1 5.6 %collective-permute-done.6.refs_4_ = bf16[8,2,64,128]{3,2,1,0:T(8,128)(2,1)S(1)} collective-permute-done((bf16[8,2,64,128]{3,2,1,0:T(8,128)(2,1)S(1)}, bf16[8,2,64,128]{3,2,1,0:T(8,128)(2,1)S(1)}, u32[]{:S(2)}, u32[]{:S(2)}) %collective-permute-start.6) | collective-permute-done | bytes 262176 | tf_op jit(solution)/shard_map/ppermute | solution.py:35
  47.7 1.3 %row.1.kv = bf16[2,1024,128]{2,1,0:T(8,128)(2,1)S(1)} custom-call(s32[64]{0:T(128)S(1)} %select_reduce_fusion.tab, s32[64]{0:T(128)S(1)} %get-tuple-element.39.cs, s32[1]{0:T(128)} %copy.13.count, bf16[8,2,64,128]{3,2,1,0:T(8,128)(2,1)S(1)} %column.1.refs_0_, bf16[8,2,64,128]{3,2,1,0:T(8,128)(2,1)S(1)} %collective-permute-done.3.refs_1_, ...), custom_call_target="tpu_custom_call" | custom-call | tf_op jit(solution)/shard_map/row/pallas_call | solution.py:242
  49.1 0.8 collective-permute-start.12
  49.8 1.3 %collective-permute-start.11 = (bf16[2,1024,128]{2,1,0:T(8,128)(2,1)S(1)}, bf16[2,1024,128]{2,1,0:T(8,128)(2,1)S(1)}, u32[]{:S(2)}, u32[]{:S(2)}) collective-permute-start(bf16[2,1024,128]{2,1,0:T(8,128)(2,1)S(1)} %row.1.kv), channel_id=1, source_target_pairs={{0,24},{1,25},{2,26},{3,27},{4,28},{5,29},{6,30},{7,31},{8,0},{9,1... | collective-permute-start | bytes 1572872 | tf_op jit(solution)/shard_map/ppermute | solution.py:29
  51.2 0.4 collective-permute-start.10
  51.6 4.1 %convolution_convert_fusion.q = bf16[256,512]{1,0:T(8,128)(2,1)S(1)} fusion(bf16[4096,512]{1,0:T(8,128)(2,1)} %param.14, bf16[256,4096]{1,0:T(8,128)(2,1)} %param.12, f32[4096]{0:T(1024)S(1)} %copy-done.7, f32[256]{0:T(256)S(1)} %add_rsqrt_fusion), kind=kOutput, calls=%fused_computation.5 | convolution fusion | flops 1078067200 | bytes 6571008 | tf_op jit(solution)/shard_map/dot_general | solution.py:263
  55.8 2.2 %near.1 = (f32[4,256,128]{2,1,0:T(8,128)S(1)}, f32[4,256,128]{2,1,0:T(8,128)S(1)}, f32[4,256,128]{2,1,0:T(8,128)S(1)}) custom-call(s32[1,4]{1,0:T(1,128)S(1)} %copy-done.4, s32[1]{0:T(128)S(6)} %copy.14.cnt, bf16[256,512]{1,0:T(8,128)(2,1)S(1)} %convolution_convert_fusion.q, bf16[256,128]{1,0:T(8,128)(2,1)S(1)} %collective-permute-done.13.kp, ...), custom_call_target="tpu_custom_call" | custom-call | tf_op jit(solution)/shard_map/near/pallas_call | solution.py:266
  57.9 2.5 %far.3 = (f32[4,256,128]{2,1,0:T(8,128)S(1)}, f32[4,256,128]{2,1,0:T(8,128)S(1)}, f32[4,256,128]{2,1,0:T(8,128)S(1)}) custom-call(s32[1]{0:T(128)} %copy.13.count, bf16[256,512]{1,0:T(8,128)(2,1)S(1)} %convolution_convert_fusion.q, bf16[2,1024,128]{2,1,0:T(8,128)(2,1)S(1)} %row.1.kv, f32[4,256,128]{2,1,0:T(8,128)S(1)} %get-tuple-element.25.m_in, ...), custom_call_target="tpu_custom_call" | custom-call | tf_op jit(solution)/shard_map/far/pallas_call | solution.py:275
  60.5 3.5 %collective-permute-done.12.kv = bf16[2,1024,128]{2,1,0:T(8,128)(2,1)S(1)} collective-permute-done((bf16[2,1024,128]{2,1,0:T(8,128)(2,1)S(1)}, bf16[2,1024,128]{2,1,0:T(8,128)(2,1)S(1)}, u32[]{:S(2)}, u32[]{:S(2)}) %collective-permute-start.12) | collective-permute-done | bytes 524320 | tf_op jit(solution)/shard_map/ppermute | solution.py:29
  64.0 2.5 %far.4 = (f32[4,256,128]{2,1,0:T(8,128)S(1)}, f32[4,256,128]{2,1,0:T(8,128)S(1)}, f32[4,256,128]{2,1,0:T(8,128)S(1)}) custom-call(s32[1]{0:T(128)} %copy.13.count, bf16[256,512]{1,0:T(8,128)(2,1)S(1)} %convolution_convert_fusion.q, bf16[2,1024,128]{2,1,0:T(8,128)(2,1)S(1)} %collective-permute-done.12.kv, f32[4,256,128]{2,1,0:T(8,128)S(1)} %get-tuple-element.28.m_in, ...), custom_call_target="tpu_custom_call" | custom-call | tf_op jit(solution)/shard_map/far/pallas_call | solution.py:275
  66.5 4.7 %collective-permute-done.11.kv = bf16[2,1024,128]{2,1,0:T(8,128)(2,1)S(1)} collective-permute-done((bf16[2,1024,128]{2,1,0:T(8,128)(2,1)S(1)}, bf16[2,1024,128]{2,1,0:T(8,128)(2,1)S(1)}, u32[]{:S(2)}, u32[]{:S(2)}) %collective-permute-start.11) | collective-permute-done | bytes 524320 | tf_op jit(solution)/shard_map/ppermute | solution.py:29
  71.2 2.5 %far.5 = (f32[4,256,128]{2,1,0:T(8,128)S(1)}, f32[4,256,128]{2,1,0:T(8,128)S(1)}, f32[4,256,128]{2,1,0:T(8,128)S(1)}) custom-call(s32[1]{0:T(128)} %copy.13.count, bf16[256,512]{1,0:T(8,128)(2,1)S(1)} %convolution_convert_fusion.q, bf16[2,1024,128]{2,1,0:T(8,128)(2,1)S(1)} %collective-permute-done.11.kv, f32[4,256,128]{2,1,0:T(8,128)S(1)} %get-tuple-element.31.m_in, ...), custom_call_target="tpu_custom_call" | custom-call | tf_op jit(solution)/shard_map/far/pallas_call | solution.py:275
  73.7 2.5 %last.1.att = bf16[256,512]{1,0:T(8,128)(2,1)S(1)} custom-call(s32[1]{0:T(128)} %copy.13.count, bf16[256,512]{1,0:T(8,128)(2,1)S(1)} %convolution_convert_fusion.q, bf16[2,1024,128]{2,1,0:T(8,128)(2,1)S(1)} %collective-permute-done.10.kv, f32[4,256,128]{2,1,0:T(8,128)S(1)} %get-tuple-element.34.m_in, f32[4,256,128]{2,1,0:T(8,128)S(1)} %get-tuple-element.35.l_in, ...), custom_call_target="tpu_custom_call" | custom-call | tf_op jit(solution)/shard_map/last/pallas_call | solution.py:283
  76.3 2.0 %away.1 = bf16[4,256,512]{2,1,0:T(8,128)(2,1)S(1)} custom-call(s32[4]{0:T(128)S(1)} %add_subtract_fusion.cols, bf16[256,512]{1,0:T(8,128)(2,1)S(1)} %last.1.att, bf16[512,4096]{1,0:T(8,128)(2,1)S(1)} %copy-done.1), custom_call_target="tpu_custom_call" | custom-call | tf_op jit(solution)/shard_map/away/pallas_call | solution.py:296
  78.3 0.3 collective-permute-start.15
  78.6 2.6 %collective-permute-done.15.recv = bf16[4,256,512]{2,1,0:T(8,128)(2,1)S(1)} collective-permute-done((bf16[4,256,512]{2,1,0:T(8,128)(2,1)S(1)}, bf16[4,256,512]{2,1,0:T(8,128)(2,1)S(1)}, u32[]{:S(2)}, u32[]{:S(2)}) %collective-permute-start.15) | collective-permute-done | bytes 1048608 | tf_op jit(solution)/shard_map/ppermute | solution.py:47
  81.3 0.8 home.7
  82.1 2.8 %collective-permute-start.18 = (bf16[256,512]{1,0:T(8,128)(2,1)S(1)}, bf16[256,512]{1,0:T(8,128)(2,1)S(1)}, u32[]{:S(2)}, u32[]{:S(2)}) collective-permute-start(bf16[256,512]{1,0:T(8,128)(2,1)S(1)} %home.7), channel_id=1, source_target_pairs={{0,192},{32,224},{64,0},{96,32},{128,64},{160,96},{192,128},{224,1... | collective-permute-start | bytes 786440 | tf_op jit(solution)/shard_map/ppermute | solution.py:41
  84.9 0.8 home.6
  85.9 0.8 home.5
  86.7 2.3 %collective-permute-start.16 = (bf16[256,512]{1,0:T(8,128)(2,1)S(1)}, bf16[256,512]{1,0:T(8,128)(2,1)S(1)}, u32[]{:S(2)}, u32[]{:S(2)}) collective-permute-start(bf16[256,512]{1,0:T(8,128)(2,1)S(1)} %home.5), channel_id=1, source_target_pairs={{0,128},{32,160},{64,192},{96,224},{128,0},{160,32},{192,64},{224,... | collective-permute-start | bytes 786440 | tf_op jit(solution)/shard_map/ppermute | solution.py:41
  89.1 0.8 home.4.mine
  89.9 6.5 %collective-permute-done.18.c = bf16[256,512]{1,0:T(8,128)(2,1)S(1)} collective-permute-done((bf16[256,512]{1,0:T(8,128)(2,1)S(1)}, bf16[256,512]{1,0:T(8,128)(2,1)S(1)}, u32[]{:S(2)}, u32[]{:S(2)}) %collective-permute-start.18) | collective-permute-done | bytes 262176 | tf_op jit(solution)/shard_map/ppermute | solution.py:41
  96.5 4.3 %collective-permute-done.17.b = bf16[256,512]{1,0:T(8,128)(2,1)S(1)} collective-permute-done((bf16[256,512]{1,0:T(8,128)(2,1)S(1)}, bf16[256,512]{1,0:T(8,128)(2,1)S(1)}, u32[]{:S(2)}, u32[]{:S(2)}) %collective-permute-start.17) | collective-permute-done | bytes 262176 | tf_op jit(solution)/shard_map/ppermute | solution.py:41
  100.8 0.8 final.1
  (33 shorter events, 0.5 us)
Async XLA Ops:
  0.0 31.7 %copy-start = (bf16[4096,128]{1,0:T(8,128)(2,1)S(1)}, bf16[4096,128]{1,0:T(8,128)(2,1)}, u32[]{:S(2)}) copy-start(bf16[4096,128]{1,0:T(8,128)(2,1)} %param.15) | copy-start | bytes 3145732
  0.0 40.1 %copy-start.7 = (f32[4096]{0:T(1024)S(1)}, f32[4096]{0:T(1024)}, u32[]{:S(2)}) copy-start(f32[4096]{0:T(1024)} %param.13) | copy-start | bytes 49156
  1.8 1.0 copy-start.2
  2.7 0.9 copy-start.3
  3.7 36.4 %copy-start.5 = (bf16[256,4096]{1,0:T(8,128)(2,1)S(1)}, bf16[256,4096]{1,0:T(8,128)(2,1)}, u32[]{:S(2)}) copy-start(bf16[256,4096]{1,0:T(8,128)(2,1)} %param.12) | copy-start | bytes 6291460
  3.7 36.4 %copy-start.6 = (bf16[4096,128]{1,0:T(8,128)(2,1)S(1)}, bf16[4096,128]{1,0:T(8,128)(2,1)}, u32[]{:S(2)}) copy-start(bf16[4096,128]{1,0:T(8,128)(2,1)} %param.16) | copy-start | bytes 3145732
  4.3 4.6 %collective-permute-start = (bf16[2,2,64,128]{3,2,1,0:T(8,128)(2,1)S(1)}, bf16[2,2,64,128]{3,2,1,0:T(8,128)(2,1)S(1)}, u32[]{:S(2)}, u32[]{:S(2)}) collective-permute-start(bf16[2,2,64,128]{3,2,1,0:T(8,128)(2,1)S(1)} %get-tuple-element.22), channel_id=1, source_target_pairs={{0,8},{1,9},{2,10},{3,11},{4,12},{5,13},{6,14},{7,15},{8,16},{9,17... | collective-permute-start | bytes 196616 | tf_op jit(solution)/shard_map/ppermute | solution.py:29
  6.3 5.8 %collective-permute-start.1 = (bf16[2,2,64,128]{3,2,1,0:T(8,128)(2,1)S(1)}, bf16[2,2,64,128]{3,2,1,0:T(8,128)(2,1)S(1)}, u32[]{:S(2)}, u32[]{:S(2)}) collective-permute-start(bf16[2,2,64,128]{3,2,1,0:T(8,128)(2,1)S(1)} %get-tuple-element.23), channel_id=1, source_target_pairs={{0,16},{1,17},{2,18},{3,19},{4,20},{5,21},{6,22},{7,23},{8,24},{9,... | collective-permute-start | bytes 196616 | tf_op jit(solution)/shard_map/ppermute | solution.py:29
  7.2 5.6 %collective-permute-start.2 = (bf16[2,2,64,128]{3,2,1,0:T(8,128)(2,1)S(1)}, bf16[2,2,64,128]{3,2,1,0:T(8,128)(2,1)S(1)}, u32[]{:S(2)}, u32[]{:S(2)}) collective-permute-start(bf16[2,2,64,128]{3,2,1,0:T(8,128)(2,1)S(1)} %get-tuple-element.24), channel_id=1, source_target_pairs={{0,24},{1,25},{2,26},{3,27},{4,28},{5,29},{6,30},{7,31},{8,0},{9,1... | collective-permute-start | bytes 196616 | tf_op jit(solution)/shard_map/ppermute | solution.py:29
  13.6 10.5 %collective-permute-start.3 = (bf16[8,2,64,128]{3,2,1,0:T(8,128)(2,1)S(1)}, bf16[8,2,64,128]{3,2,1,0:T(8,128)(2,1)S(1)}, u32[]{:S(2)}, u32[]{:S(2)}) collective-permute-start(bf16[8,2,64,128]{3,2,1,0:T(8,128)(2,1)S(1)} %column.1.refs_0_), channel_id=1, source_target_pairs={{0,1},{1,2},{2,3},{3,4},{4,5},{5,6},{6,7},{7,0},{8,9},{9,10},{10,1... | collective-permute-start | bytes 786440 | tf_op jit(solution)/shard_map/ppermute | solution.py:35
  15.5 10.7 %collective-permute-start.7 = (bf16[8,2,64,128]{3,2,1,0:T(8,128)(2,1)S(1)}, bf16[8,2,64,128]{3,2,1,0:T(8,128)(2,1)S(1)}, u32[]{:S(2)}, u32[]{:S(2)}) collective-permute-start(bf16[8,2,64,128]{3,2,1,0:T(8,128)(2,1)S(1)} %column.1.refs_0_), channel_id=1, source_target_pairs={{0,7},{1,0},{2,1},{3,2},{4,3},{5,4},{6,5},{7,6},{8,15},{9,8},{10,9... | collective-permute-start | bytes 786440 | tf_op jit(solution)/shard_map/ppermute | solution.py:35
  24.1 7.6 %collective-permute-start.4 = (bf16[8,2,64,128]{3,2,1,0:T(8,128)(2,1)S(1)}, bf16[8,2,64,128]{3,2,1,0:T(8,128)(2,1)S(1)}, u32[]{:S(2)}, u32[]{:S(2)}) collective-permute-start(bf16[8,2,64,128]{3,2,1,0:T(8,128)(2,1)S(1)} %collective-permute-done.3.refs_1_), channel_id=1, source_target_pairs={{0,1},{1,2},{2,3},{3,4},{4,5},{5,6},{6,7},{7,0},{8,9},{9,10},{10,1... | collective-permute-start | bytes 786440 | tf_op jit(solution)/shard_map/ppermute | solution.py:35
  26.2 8.0 %collective-permute-start.8 = (bf16[8,2,64,128]{3,2,1,0:T(8,128)(2,1)S(1)}, bf16[8,2,64,128]{3,2,1,0:T(8,128)(2,1)S(1)}, u32[]{:S(2)}, u32[]{:S(2)}) collective-permute-start(bf16[8,2,64,128]{3,2,1,0:T(8,128)(2,1)S(1)} %collective-permute-done.7.refs_7_), channel_id=1, source_target_pairs={{0,7},{1,0},{2,1},{3,2},{4,3},{5,4},{6,5},{7,6},{8,15},{9,8},{10,9... | collective-permute-start | bytes 786440 | tf_op jit(solution)/shard_map/ppermute | solution.py:35
  31.7 8.4 %collective-permute-start.5 = (bf16[8,2,64,128]{3,2,1,0:T(8,128)(2,1)S(1)}, bf16[8,2,64,128]{3,2,1,0:T(8,128)(2,1)S(1)}, u32[]{:S(2)}, u32[]{:S(2)}) collective-permute-start(bf16[8,2,64,128]{3,2,1,0:T(8,128)(2,1)S(1)} %collective-permute-done.4.refs_2_), channel_id=1, source_target_pairs={{0,1},{1,2},{2,3},{3,4},{4,5},{5,6},{6,7},{7,0},{8,9},{9,10},{10,1... | collective-permute-start | bytes 786440 | tf_op jit(solution)/shard_map/ppermute | solution.py:35
  34.1 21.7 %collective-permute-start.13 = (bf16[256,128]{1,0:T(8,128)(2,1)S(1)}, bf16[256,128]{1,0:T(8,128)(2,1)S(1)}, u32[]{:S(2)}, u32[]{:S(2)}) collective-permute-start(bf16[256,128]{1,0:T(8,128)(2,1)S(1)} %convolution_convert_fusion.2.k), channel_id=1, source_target_pairs={{0,1},{1,2},{2,3},{3,4},{4,5},{5,6},{6,7},{7,8},{8,9},{9,10},{10,1... | collective-permute-start | bytes 196616 | tf_op jit(solution)/shard_map/ppermute | solution.py:262
  34.2 7.9 %collective-permute-start.9 = (bf16[8,2,64,128]{3,2,1,0:T(8,128)(2,1)S(1)}, bf16[8,2,64,128]{3,2,1,0:T(8,128)(2,1)S(1)}, u32[]{:S(2)}, u32[]{:S(2)}) collective-permute-start(bf16[8,2,64,128]{3,2,1,0:T(8,128)(2,1)S(1)} %collective-permute-done.8.refs_6_), channel_id=1, source_target_pairs={{0,7},{1,0},{2,1},{3,2},{4,3},{5,4},{6,5},{7,6},{8,15},{9,8},{10,9... | collective-permute-start | bytes 786440 | tf_op jit(solution)/shard_map/ppermute | solution.py:35
  40.1 7.6 %collective-permute-start.6 = (bf16[8,2,64,128]{3,2,1,0:T(8,128)(2,1)S(1)}, bf16[8,2,64,128]{3,2,1,0:T(8,128)(2,1)S(1)}, u32[]{:S(2)}, u32[]{:S(2)}) collective-permute-start(bf16[8,2,64,128]{3,2,1,0:T(8,128)(2,1)S(1)} %collective-permute-done.5.refs_3_), channel_id=1, source_target_pairs={{0,1},{1,2},{2,3},{3,4},{4,5},{5,6},{6,7},{7,0},{8,9},{9,10},{10,1... | collective-permute-start | bytes 786440 | tf_op jit(solution)/shard_map/ppermute | solution.py:35
  41.0 14.8 %collective-permute-start.14 = (bf16[256,128]{1,0:T(8,128)(2,1)S(1)}, bf16[256,128]{1,0:T(8,128)(2,1)S(1)}, u32[]{:S(2)}, u32[]{:S(2)}) collective-permute-start(bf16[256,128]{1,0:T(8,128)(2,1)S(1)} %convolution_convert_fusion.1.v), channel_id=1, source_target_pairs={{0,1},{1,2},{2,3},{3,4},{4,5},{5,6},{6,7},{7,8},{8,9},{9,10},{10,1... | collective-permute-start | bytes 196616 | tf_op jit(solution)/shard_map/ppermute | solution.py:262
  49.0 6.7 %copy-start.4 = (s32[1,4]{1,0:T(1,128)S(1)}, s32[1,4]{1,0:T(1,128)}, u32[]{:S(2)}) copy-start(s32[1,4]{1,0:T(1,128)} %offs.1) | copy-start | bytes 52
  49.1 14.9 %collective-permute-start.12 = (bf16[2,1024,128]{2,1,0:T(8,128)(2,1)S(1)}, bf16[2,1024,128]{2,1,0:T(8,128)(2,1)S(1)}, u32[]{:S(2)}, u32[]{:S(2)}) collective-permute-start(bf16[2,1024,128]{2,1,0:T(8,128)(2,1)S(1)} %row.1.kv), channel_id=1, source_target_pairs={{0,8},{1,9},{2,10},{3,11},{4,12},{5,13},{6,14},{7,15},{8,16},{9,17... | collective-permute-start | bytes 1572872 | tf_op jit(solution)/shard_map/ppermute | solution.py:29
  49.8 21.4 %collective-permute-start.11 = (bf16[2,1024,128]{2,1,0:T(8,128)(2,1)S(1)}, bf16[2,1024,128]{2,1,0:T(8,128)(2,1)S(1)}, u32[]{:S(2)}, u32[]{:S(2)}) collective-permute-start(bf16[2,1024,128]{2,1,0:T(8,128)(2,1)S(1)} %row.1.kv), channel_id=1, source_target_pairs={{0,24},{1,25},{2,26},{3,27},{4,28},{5,29},{6,30},{7,31},{8,0},{9,1... | collective-permute-start | bytes 1572872 | tf_op jit(solution)/shard_map/ppermute | solution.py:29
  51.2 22.6 %collective-permute-start.10 = (bf16[2,1024,128]{2,1,0:T(8,128)(2,1)S(1)}, bf16[2,1024,128]{2,1,0:T(8,128)(2,1)S(1)}, u32[]{:S(2)}, u32[]{:S(2)}) collective-permute-start(bf16[2,1024,128]{2,1,0:T(8,128)(2,1)S(1)} %row.1.kv), channel_id=1, source_target_pairs={{0,16},{1,17},{2,18},{3,19},{4,20},{5,21},{6,22},{7,23},{8,24},{9,... | collective-permute-start | bytes 1572872 | tf_op jit(solution)/shard_map/ppermute | solution.py:29
  60.5 15.8 %copy-start.1 = (bf16[512,4096]{1,0:T(8,128)(2,1)S(1)}, bf16[512,4096]{1,0:T(8,128)(2,1)}, u32[]{:S(2)}) copy-start(bf16[512,4096]{1,0:T(8,128)(2,1)} %w.9) | copy-start | bytes 12582916
  78.3 3.0 %collective-permute-start.15 = (bf16[4,256,512]{2,1,0:T(8,128)(2,1)S(1)}, bf16[4,256,512]{2,1,0:T(8,128)(2,1)S(1)}, u32[]{:S(2)}, u32[]{:S(2)}) collective-permute-start(bf16[4,256,512]{2,1,0:T(8,128)(2,1)S(1)} %away.1), channel_id=1, source_target_pairs={{0,32},{32,0},{64,96},{96,64},{128,160},{160,128},{192,224},{224,1... | collective-permute-start | bytes 3145736 | tf_op jit(solution)/shard_map/ppermute | solution.py:47
  82.1 14.3 %collective-permute-start.18 = (bf16[256,512]{1,0:T(8,128)(2,1)S(1)}, bf16[256,512]{1,0:T(8,128)(2,1)S(1)}, u32[]{:S(2)}, u32[]{:S(2)}) collective-permute-start(bf16[256,512]{1,0:T(8,128)(2,1)S(1)} %home.7), channel_id=1, source_target_pairs={{0,192},{32,224},{64,0},{96,32},{128,64},{160,96},{192,128},{224,1... | collective-permute-start | bytes 786440 | tf_op jit(solution)/shard_map/ppermute | solution.py:41
  85.8 15.0 %collective-permute-start.17 = (bf16[256,512]{1,0:T(8,128)(2,1)S(1)}, bf16[256,512]{1,0:T(8,128)(2,1)S(1)}, u32[]{:S(2)}, u32[]{:S(2)}) collective-permute-start(bf16[256,512]{1,0:T(8,128)(2,1)S(1)} %home.6), channel_id=1, source_target_pairs={{0,64},{32,96},{64,128},{96,160},{128,192},{160,224},{192,0},{224,... | collective-permute-start | bytes 786440 | tf_op jit(solution)/shard_map/ppermute | solution.py:41
  86.7 14.0 %collective-permute-start.16 = (bf16[256,512]{1,0:T(8,128)(2,1)S(1)}, bf16[256,512]{1,0:T(8,128)(2,1)S(1)}, u32[]{:S(2)}, u32[]{:S(2)}) collective-permute-start(bf16[256,512]{1,0:T(8,128)(2,1)S(1)} %home.5), channel_id=1, source_target_pairs={{0,128},{32,160},{64,192},{96,224},{128,0},{160,32},{192,64},{224,... | collective-permute-start | bytes 786440 | tf_op jit(solution)/shard_map/ppermute | solution.py:41

commit v2 on v1

v2 whole, which is shorter than its diff:
```python
import functools
import math

import jax
import jax.numpy as jnp
from jax import lax
from jax.experimental import pallas as pl
from jax.experimental.pallas import tpu as pltpu
from jax.sharding import PartitionSpec as P

BLK = 64
HD = 128
GROUP = 4
NY = 4
NZ = 8
NX = 4
VMEM = pltpu.VMEM
VSPEC = pl.BlockSpec(memory_space=pltpu.VMEM)
SSPEC = pl.BlockSpec(memory_space=pltpu.SMEM)
SCALE2 = math.log2(math.e) / math.sqrt(HD)
NEG = -jnp.inf


def params(mib):
    return pltpu.CompilerParams(vmem_limit_bytes=mib << 20)


def cost(us):
    return pl.CostEstimate(flops=int(us * 1e9), bytes_accessed=0, transcendentals=0)


def tie(*values):
    return lax.optimization_barrier(values)


def shift_y(block, d):
    return lax.ppermute(
        block, "seq", [(y * NZ + z, (y + d) % NY * NZ + z) for y in range(NY) for z in range(NZ)]
    )


def shift_z(block, d):
    return lax.ppermute(
        block, "seq", [(y * NZ + z, y * NZ + (z + d) % NZ) for y in range(NY) for z in range(NZ)]
    )


def shift_x(block, d):
    return lax.ppermute(
        block, "heads", [(2 * x + c, 2 * ((x + d) % NX) + c) for x in range(NX) for c in range(2)]
    )


def swap_core(block):
    return lax.ppermute(block, "heads", [(i, i ^ 1) for i in range(2 * NX)])


def position():
    me = lax.axis_index("seq")
    return me // NZ, lax.rem(me, NZ)


def at(tab, group):
    return tab[64 + group]


def pick_kernel(tab, ck, cv, *outs):
    y, z = position()
    group = z * NY + y
    start = at(tab, group)
    size = at(tab, group + 1) - start
    for dy in range(NY):
        for j in range(2):
            i = ((y + dy - start) & 3) + 4 * j
            entry = tab[jnp.minimum(start + i, 63)]
            row = pl.multiple_of(jnp.where(i < size, entry & 15, 0) * BLK, BLK)
            outs[dy][j, 0] = ck[0, pl.ds(row, BLK), :]
            outs[dy][j, 1] = cv[0, pl.ds(row, BLK), :]


def column_kernel(tab, r0, r1, r2, r3, out):
    y, z = position()
    recv = (r0, r1, r2, r3)
    start = at(tab, z * NY)
    size = at(tab, z * NY + NY) - start
    first = (y - start) & 3
    for i in range(8):
        off = first + 4 * i
        live = off < size
        r = jnp.minimum(start + off, 63)
        hy = (tab[r] >> 4) & 3
        j = jnp.where(live, (r - at(tab, z * NY + hy)) >> 2, 0)
        d = jnp.where(live, (y - hy) & 3, 0)
        for k in range(NY):

            @pl.when(d == k)
            def _():
                out[i] = recv[k][j]


def row_kernel(tab, *refs):
    y, z = position()
    recv, outs = refs[:NZ], refs[NZ:]
    for m in range(16):
        r = y + 4 * m
        live = r < at(tab, 32)
        zs = jnp.where(live, tab[r] >> 6, z)
        start = at(tab, zs * NY)
        first = (y - start) & 3
        i = jnp.where(live, (r - start - first) >> 2, 0)
        d = (z - zs) & 7
        out, place = outs[m // 8], m % 8 * BLK
        for k in range(NZ):

            @pl.when(d == k)
            def _():
                out[0, place : place + BLK] = recv[k][i, 0]
                out[1, place : place + BLK] = recv[k][i, 1]


def near_kernel(offs, cnt, q, kp, vp, k, v, m_out, l_out, acc_out):
    me = lax.axis_index("seq")
    rows = k.shape[0]
    keys = jnp.concatenate([kp[...], k[...]], axis=0)
    values = jnp.concatenate([vp[...], v[...]], axis=0)
    t = lax.broadcasted_iota(jnp.int32, (rows, 2 * rows), 0)
    u = lax.broadcasted_iota(jnp.int32, (rows, 2 * rows), 1) - rows
    gap = (t >> 6) - (u >> 6)
    hit = (gap == 0) & (u <= t)
    for e in range(4):
        off = jnp.where((e < cnt[0]) & (offs[0, e] >= 0), offs[0, e], -100)
        hit = hit | (gap == off)
    hit = hit & (u >= jnp.where(me > 0, -rows, 0))
    for h in range(GROUP):
        s = lax.dot_general(
            q[:, h * HD : (h + 1) * HD],
            keys,
            (((1,), (1,)), ((), ())),
            preferred_element_type=jnp.float32,
        )
        s = jnp.where(hit, s, NEG)
        top = jnp.max(s, axis=1, keepdims=True)
        p = jnp.exp2((s - top) * SCALE2)
        m_out[h] = jnp.broadcast_to(top, (rows, HD))
        l_out[h] = jnp.broadcast_to(jnp.sum(p, axis=1, keepdims=True), (rows, HD))
        acc_out[h] = jnp.dot(p.astype(jnp.bfloat16), values, preferred_element_type=jnp.float32)


def far_step(live, q, lo, hi, m_in, l_in, acc_in, h):
    def scores(kv, base):
        s = lax.dot_general(
            q[:, h * HD : (h + 1) * HD],
            kv[0],
            (((1,), (1,)), ((), ())),
            preferred_element_type=jnp.float32,
        )
        key = base + lax.broadcasted_iota(jnp.int32, s.shape, 1)
        return jnp.where(key < live, s, NEG)

    s0, s1 = scores(lo, 0), scores(hi, lo.shape[1])
    old = m_in[h][:, :1]
    top = jnp.maximum(
        old,
        jnp.maximum(jnp.max(s0, axis=1, keepdims=True), jnp.max(s1, axis=1, keepdims=True)),
    )
    factor = jnp.exp2((old - top) * SCALE2)
    p0 = jnp.exp2((s0 - top) * SCALE2)
    p1 = jnp.exp2((s1 - top) * SCALE2)
    total = (
        l_in[h][:, :1] * factor
        + jnp.sum(p0, axis=1, keepdims=True)
        + jnp.sum(p1, axis=1, keepdims=True)
    )
    acc = (
        acc_in[h] * factor
        + jnp.dot(p0.astype(jnp.bfloat16), lo[1], preferred_element_type=jnp.float32)
        + jnp.dot(p1.astype(jnp.bfloat16), hi[1], preferred_element_type=jnp.float32)
    )
    return top, total, acc


def live_keys(tab, shift):
    y, _ = position()
    return ((at(tab, 32) - ((y - shift) & 3) + 3) >> 2) * BLK


def far_kernel(shift, tab, q, lo, hi, m_in, l_in, acc_in, m_out, l_out, acc_out):
    live = live_keys(tab, shift)
    for h in range(GROUP):
        top, total, acc = far_step(live, q, lo, hi, m_in, l_in, acc_in, h)
        m_out[h] = jnp.broadcast_to(top, m_out.shape[1:])
        l_out[h] = jnp.broadcast_to(total, l_out.shape[1:])
        acc_out[h] = acc


def last_kernel(shift, tab, q, lo, hi, m_in, l_in, acc_in, att):
    live = live_keys(tab, shift)
    for h in range(GROUP):
        _, total, acc = far_step(live, q, lo, hi, m_in, l_in, acc_in, h)
        att[:, h * HD : (h + 1) * HD] = (acc / total).astype(jnp.bfloat16)


def away_kernel(cols, att, w, out):
    out[0] = jnp.dot(att[...], w[...], preferred_element_type=jnp.float32).astype(out.dtype)


def home_kernel(cols, att, w, recv, out):
    mine = jnp.dot(att[...], w[...], preferred_element_type=jnp.float32)
    out[0] = mine + recv[0].astype(jnp.float32)


def halves_kernel(cols, att, w, recv, a, b):
    mine = jnp.dot(att[...], w[...], preferred_element_type=jnp.float32)
    total = (mine + recv[0].astype(jnp.float32)).astype(a.dtype)
    half = a.shape[0]
    a[...] = total[:half]
    b[...] = total[half:]


def pass_kernel(home, a, b, right, left):
    half = a.shape[0]
    right[:half] = (home[1, :half] + a[...].astype(jnp.float32)).astype(right.dtype)
    right[half:] = home[1, half:].astype(right.dtype)
    left[:half] = home[2, :half].astype(left.dtype)
    left[half:] = (home[2, half:] + b[...].astype(jnp.float32)).astype(left.dtype)


def final_kernel(home, a, b, out):
    total = home[0] + a[...].astype(jnp.float32) + b[...].astype(jnp.float32)
    out[...] = total.astype(out.dtype)


def local(
    tokens,
    norm_gain,
    w_query,
    w_key,
    w_value,
    w_out,
    cache_keys,
    cache_values,
    vert_blocks,
    vert_count,
    slash_offsets,
    slash_count,
):
    rows = tokens.shape[0]
    bf16 = jnp.bfloat16
    f32 = jnp.float32
    blocks = vert_blocks[0]
    index = jnp.arange(128, dtype=jnp.int32)
    entry = index[:64]
    key = jnp.where(
        entry < vert_count[0],
        (((blocks >> 4) & 7) << 6) | ((blocks >> 7) << 4) | (blocks & 15),
        4096 + entry,
    )
    edges = jnp.concatenate([key, entry * 16])
    below = jnp.sum((key[None, :] < edges[:, None]).astype(jnp.int32), axis=1)
    ranked = jnp.sum(jnp.where(below[None, :64] == index[:, None], key[None, :], 0), axis=1)
    tab = jnp.where(index < 64, ranked, below)

    slot = jax.ShapeDtypeStruct((2, 2, BLK, HD), bf16)
    picked = pl.pallas_call(
        pick_kernel,
        out_shape=[slot] * NY,
        in_specs=[SSPEC, VSPEC, VSPEC],
        out_specs=[VSPEC] * NY,
        compiler_params=params(8),
        cost_estimate=cost(0.7),
        name="pick",
    )(tab, cache_keys, cache_values)
    spread = [picked[0]] + [shift_y(picked[d], d) for d in range(1, NY)]
    activation = tokens.astype(f32)
    normed = (
        activation
        * lax.rsqrt(jnp.mean(activation * activation, axis=-1, keepdims=True) + 1e-05)
        * norm_gain
    ).astype(bf16)
    spread[3], normed = tie(spread[3], normed)
    column = pl.pallas_call(
        column_kernel,
        out_shape=jax.ShapeDtypeStruct((8, 2, BLK, HD), bf16),
        in_specs=[SSPEC] + [VSPEC] * NY,
        out_specs=VSPEC,
        compiler_params=params(8),
        cost_estimate=cost(0.8),
        name="column",
    )(tab, *spread)
    key_rows = jnp.dot(normed, w_key, preferred_element_type=f32).astype(bf16)
    value_rows = jnp.dot(normed, w_value, preferred_element_type=f32).astype(bf16)
    seqs = lax.axis_size("seq")
    route = [(i, (i + 1) % seqs) for i in range(seqs)]
    ring = [column] + [None] * 7
    ring[1], ring[7] = shift_z(column, 1), shift_z(column, -1)
    ring[1], key_rows, value_rows = tie(ring[1], key_rows, value_rows)
    ring[2], ring[6] = shift_z(ring[1], 1), shift_z(ring[7], -1)
    before_keys, before_values = lax.ppermute((key_rows, value_rows), "seq", route)
    queries = jnp.dot(normed, w_query, preferred_element_type=f32).astype(bf16)
    ring[2], queries = tie(ring[2], queries)
    ring[3], ring[5] = shift_z(ring[2], 1), shift_z(ring[6], -1)
    state_shape = [jax.ShapeDtypeStruct((GROUP, rows, HD), f32)] * 3
    state = pl.pallas_call(
        near_kernel,
        out_shape=state_shape,
        in_specs=[SSPEC] * 2 + [VSPEC] * 5,
        out_specs=[VSPEC] * 3,
        compiler_params=params(24),
        cost_estimate=cost(2.2),
        name="near",
    )(slash_offsets, slash_count, queries, before_keys, before_values, key_rows, value_rows)
    ring[4] = shift_z(ring[3], 1)
    ring[4], *state = tie(ring[4], *state)
    half = jax.ShapeDtypeStruct((2, 8 * BLK, HD), bf16)
    own = pl.pallas_call(
        row_kernel,
        out_shape=[half] * 2,
        in_specs=[SSPEC] + [VSPEC] * NZ,
        out_specs=[VSPEC] * 2,
        compiler_params=params(16),
        cost_estimate=cost(1.3),
        name="row",
    )(tab, *ring)
    lo1, hi3 = shift_y(own[0], 1), shift_y(own[1], -1)
    hi1, lo3 = shift_y(own[1], 1), shift_y(own[0], -1)
    lo2, hi2 = shift_y(lo1, 1), shift_y(hi3, -1)
    for shift, part in ((0, own), (1, (lo1, hi1)), (3, (lo3, hi3))):
        state = pl.pallas_call(
            functools.partial(far_kernel, shift),
            out_shape=state_shape,
            in_specs=[SSPEC] + [VSPEC] * 6,
            out_specs=[VSPEC] * 3,
            compiler_params=params(24),
            cost_estimate=cost(2.5),
            name="far",
        )(tab, queries, *part, *state)
    attended = pl.pallas_call(
        functools.partial(last_kernel, 2),
        out_shape=jax.ShapeDtypeStruct((rows, GROUP * HD), bf16),
        in_specs=[SSPEC] + [VSPEC] * 6,
        out_specs=VSPEC,
        compiler_params=params(24),
        cost_estimate=cost(2.5),
        name="last",
    )(tab, queries, lo2, hi2, *state)

    heads = lax.axis_index("heads")
    x, core = heads // 2, lax.rem(heads, 2)
    depth = GROUP * HD
    order = (x + jnp.arange(NX, dtype=jnp.int32)) & 3
    away_cols, home_cols = order * 2 + 1 - core, order * 2 + core
    att_spec = pl.BlockSpec((rows, depth), lambda i, cols: (0, 0))
    pieces = (0, 1, 3)

    def pick_piece(i, seq):
        return seq[0] if len(seq) == 1 else jnp.where(i == 2, seq[-1], i)

    def w_spec(seq):
        return pl.BlockSpec((depth, depth), lambda i, cols: (0, cols[pick_piece(i, seq)]))

    def piece_spec():
        return pl.BlockSpec((1, rows, depth), lambda i, cols: (i, 0, 0))

    def away(seq):
        return pl.pallas_call(
            away_kernel,
            out_shape=jax.ShapeDtypeStruct((len(seq), rows, depth), bf16),
            grid_spec=pltpu.PrefetchScalarGridSpec(
                num_scalar_prefetch=1,
                grid=(len(seq),),
                in_specs=[att_spec, w_spec(seq)],
                out_specs=piece_spec(),
            ),
            compiler_params=params(16),
            cost_estimate=cost(0.5 * len(seq)),
            name="away",
        )(away_cols, attended, w_out)

    recv_two = swap_core(away((2,)))
    recv = swap_core(away(pieces))
    upper, lower = pl.pallas_call(
        halves_kernel,
        out_shape=[jax.ShapeDtypeStruct((rows // 2, depth), bf16)] * 2,
        grid_spec=pltpu.PrefetchScalarGridSpec(
            num_scalar_prefetch=1,
            grid=(1,),
            in_specs=[att_spec, w_spec((2,)), piece_spec()],
            out_specs=[pl.BlockSpec((rows // 2, depth), lambda i, cols: (0, 0))] * 2,
        ),
        compiler_params=params(16),
        cost_estimate=cost(0.8),
        name="halves",
    )(home_cols, attended, w_out, recv_two)
    upper, lower = shift_x(upper, 1), shift_x(lower, -1)
    home = pl.pallas_call(
        home_kernel,
        out_shape=jax.ShapeDtypeStruct((3, rows, depth), f32),
        grid_spec=pltpu.PrefetchScalarGridSpec(
            num_scalar_prefetch=1,
            grid=(3,),
            in_specs=[att_spec, w_spec(pieces), piece_spec()],
            out_specs=piece_spec(),
        ),
        compiler_params=params(16),
        cost_estimate=cost(1.5),
        name="home",
    )(home_cols, attended, w_out, recv)
    right, left = pl.pallas_call(
        pass_kernel,
        out_shape=[jax.ShapeDtypeStruct((rows, depth), bf16)] * 2,
        in_specs=[VSPEC] * 3,
        out_specs=[VSPEC] * 2,
        compiler_params=params(16),
        cost_estimate=cost(0.6),
        name="pass",
    )(home, upper, lower)
    return pl.pallas_call(
        final_kernel,
        out_shape=jax.ShapeDtypeStruct((rows, depth), bf16),
        in_specs=[VSPEC] * 3,
        out_specs=VSPEC,
        compiler_params=params(16),
        cost_estimate=cost(0.6),
        name="final",
    )(home, shift_x(right, 1), shift_x(left, -1))


def solution(mesh):
    return jax.shard_map(
        local,
        mesh=mesh,
        in_specs=(
            P("seq", None),
            P(),
            P(None, "heads"),
            P(None, "heads"),
            P(None, "heads"),
            P("heads", None),
            P("heads", "seq", None),
            P("heads", "seq", None),
            P("heads", None),
            P("heads"),
            P("heads", None),
            P("heads"),
        ),
        out_specs=P("seq", "heads"),
        check_vma=False,
    )
```

time: 102 us -> 99.5 us (0.975)
  the two profiles are of different devices: /device:TPU:24 before, /device:TPU:6 now
where the time goes in v2:
time: 99.5 us; the launch traced here: 99.3 us
  waiting for transfers between devices  33.3 us (33%)
  starting transfers between devices  32.7 us (33%)
  Pallas kernels  23.2 us (23%)
  matrix products  3.38 us (3%)
  local copies, waits for them, and re-layouts  2.89 us (3%)
  other arithmetic  2.1 us (2%)
  between operations  1.65 us (2%)
    ppermute x9, starting transfers between devices, shift_y(): lax.ppermute(block, 'seq', [(y * NZ + z, (y + d) % NY * NZ + z) for y in...  15.1 us
    ppermute x7, waiting for transfers between devices, shift_z(): lax.ppermute(block, 'seq', [(y * NZ + z, y * NZ + (z + d) % NZ) for y in...  14 us
    ppermute x7, starting transfers between devices, shift_z(): lax.ppermute(block, 'seq', [(y * NZ + z, y * NZ + (z + d) % NZ) for y in...  12.8 us
    ppermute x4, waiting for transfers between devices, shift_x(): lax.ppermute(block, 'heads', [(2 * x + c, 2 * ((x + d) % NX) + c) for x i...  10.4 us
    pallas_call x3, Pallas kernels, local(): pl.pallas_call(functools.partial(far_kernel, shift), out_shape=state_shap...  9.39 us
    ppermute x9, waiting for transfers between devices, shift_y(): lax.ppermute(block, 'seq', [(y * NZ + z, (y + d) % NY * NZ + z) for y in...  6.65 us
    ppermute x4, starting transfers between devices, shift_x(): lax.ppermute(block, 'heads', [(2 * x + c, 2 * ((x + d) % NX) + c) for x i...  4.21 us
    pallas_call x1, Pallas kernels, local(): pl.pallas_call(functools.partial(last_kernel, 2), out_shape=jax.ShapeDtyp...  3.12 us
  transfers between devices with their start and end apart: 24, of which 11 were waited for; matrix products, arithmetic and copies ran while one was open for 5% of the time, Pallas kernels for 15%

profile of v2, /device:TPU:6, one launch (start us, length us, event | category | flops | bytes accessed | tf_op | source)
XLA Modules:
  0.0 99.3 jit_solution(1693657360407588421)
XLA Ops:
  0.8 0.7 compare_select_fusion
  1.7 0.9 copy-done.2
  2.7 0.9 copy-done.3
  3.6 0.6 pick.1
  4.2 3.1 %collective-permute-start.2 = (bf16[2,2,64,128]{3,2,1,0:T(8,128)(2,1)S(1)}, bf16[2,2,64,128]{3,2,1,0:T(8,128)(2,1)S(1)}, u32[]{:S(2)}, u32[]{:S(2)}) collective-permute-start(bf16[2,2,64,128]{3,2,1,0:T(8,128)(2,1)S(1)} %get-tuple-element.41), channel_id=1, source_target_pairs={{0,24},{1,25},{2,26},{3,27},{4,28},{5,29},{6,30},{7,31},{8,0},{9,1... | collective-permute-start | bytes 196616 | tf_op jit(solution)/shard_map/ppermute | solution.py:37
  7.3 2.2 %collective-permute-start.1 = (bf16[2,2,64,128]{3,2,1,0:T(8,128)(2,1)S(1)}, bf16[2,2,64,128]{3,2,1,0:T(8,128)(2,1)S(1)}, u32[]{:S(2)}, u32[]{:S(2)}) collective-permute-start(bf16[2,2,64,128]{3,2,1,0:T(8,128)(2,1)S(1)} %get-tuple-element.40), channel_id=1, source_target_pairs={{0,16},{1,17},{2,18},{3,19},{4,20},{5,21},{6,22},{7,23},{8,24},{9,... | collective-permute-start | bytes 196616 | tf_op jit(solution)/shard_map/ppermute | solution.py:37
  9.5 0.5 fusion
  10.0 0.6 fusion.2
  10.7 2.9 %collective-permute-done.r1 = bf16[2,2,64,128]{3,2,1,0:T(8,128)(2,1)S(1)} collective-permute-done((bf16[2,2,64,128]{3,2,1,0:T(8,128)(2,1)S(1)}, bf16[2,2,64,128]{3,2,1,0:T(8,128)(2,1)S(1)}, u32[]{:S(2)}, u32[]{:S(2)}) %collective-permute-start) | collective-permute-done | bytes 65568 | tf_op jit(solution)/shard_map/ppermute | solution.py:37
  13.6 0.8 column.1.refs_0_
  14.4 2.0 %collective-permute-start.3 = (bf16[8,2,64,128]{3,2,1,0:T(8,128)(2,1)S(1)}, bf16[8,2,64,128]{3,2,1,0:T(8,128)(2,1)S(1)}, u32[]{:S(2)}, u32[]{:S(2)}) collective-permute-start(bf16[8,2,64,128]{3,2,1,0:T(8,128)(2,1)S(1)} %column.1.refs_0_), channel_id=1, source_target_pairs={{0,1},{1,2},{2,3},{3,4},{4,5},{5,6},{6,7},{7,0},{8,9},{9,10},{10,1... | collective-permute-start | bytes 786440 | tf_op jit(solution)/shard_map/ppermute | solution.py:43
  16.4 4.0 %collective-permute-start.9 = (bf16[8,2,64,128]{3,2,1,0:T(8,128)(2,1)S(1)}, bf16[8,2,64,128]{3,2,1,0:T(8,128)(2,1)S(1)}, u32[]{:S(2)}, u32[]{:S(2)}) collective-permute-start(bf16[8,2,64,128]{3,2,1,0:T(8,128)(2,1)S(1)} %column.1.refs_0_), channel_id=1, source_target_pairs={{0,7},{1,0},{2,1},{3,2},{4,3},{5,4},{6,5},{7,6},{8,15},{9,8},{10,9... | collective-permute-start | bytes 786440 | tf_op jit(solution)/shard_map/ppermute | solution.py:43
  20.4 0.7 convolution_convert_fusion.1.v
  21.2 0.7 convolution_convert_fusion.2.k
  21.9 3.4 %collective-permute-done.3.refs_1_ = bf16[8,2,64,128]{3,2,1,0:T(8,128)(2,1)S(1)} collective-permute-done((bf16[8,2,64,128]{3,2,1,0:T(8,128)(2,1)S(1)}, bf16[8,2,64,128]{3,2,1,0:T(8,128)(2,1)S(1)}, u32[]{:S(2)}, u32[]{:S(2)}) %collective-permute-start.3) | collective-permute-done | bytes 262176 | tf_op jit(solution)/shard_map/ppermute | solution.py:43
  25.3 1.9 %convolution_convert_fusion.q = bf16[256,512]{1,0:T(8,128)(2,1)} fusion(bf16[256,4096]{1,0:T(8,128)(2,1)S(1)} %fusion.2, bf16[4096,512]{1,0:T(8,128)(2,1)S(1)} %copy-done.10), kind=kOutput, calls=%fused_computation.5 | convolution fusion | flops 1073872896 | bytes 6553600 | tf_op jit(solution)/shard_map/dot_general | solution.py:299
  27.3 5.6 %collective-permute-done.4.refs_2_ = bf16[8,2,64,128]{3,2,1,0:T(8,128)(2,1)S(1)} collective-permute-done((bf16[8,2,64,128]{3,2,1,0:T(8,128)(2,1)S(1)}, bf16[8,2,64,128]{3,2,1,0:T(8,128)(2,1)S(1)}, u32[]{:S(2)}, u32[]{:S(2)}) %collective-permute-start.4) | collective-permute-done | bytes 262176 | tf_op jit(solution)/shard_map/ppermute | solution.py:43
  32.9 3.2 %collective-permute-start.10 = (bf16[8,2,64,128]{3,2,1,0:T(8,128)(2,1)S(1)}, bf16[8,2,64,128]{3,2,1,0:T(8,128)(2,1)S(1)}, u32[]{:S(2)}, u32[]{:S(2)}) collective-permute-start(bf16[8,2,64,128]{3,2,1,0:T(8,128)(2,1)S(1)} %collective-permute-done.9.refs_7_), channel_id=1, source_target_pairs={{0,7},{1,0},{2,1},{3,2},{4,3},{5,4},{6,5},{7,6},{8,15},{9,8},{10,9... | collective-permute-start | bytes 786440 | tf_op jit(solution)/shard_map/ppermute | solution.py:43
  36.2 4.9 %collective-permute-done.5.refs_3_ = bf16[8,2,64,128]{3,2,1,0:T(8,128)(2,1)S(1)} collective-permute-done((bf16[8,2,64,128]{3,2,1,0:T(8,128)(2,1)S(1)}, bf16[8,2,64,128]{3,2,1,0:T(8,128)(2,1)S(1)}, u32[]{:S(2)}, u32[]{:S(2)}) %collective-permute-start.5) | collective-permute-done | bytes 262176 | tf_op jit(solution)/shard_map/ppermute | solution.py:43
  41.1 3.5 %collective-permute-start.11 = (bf16[8,2,64,128]{3,2,1,0:T(8,128)(2,1)S(1)}, bf16[8,2,64,128]{3,2,1,0:T(8,128)(2,1)S(1)}, u32[]{:S(2)}, u32[]{:S(2)}) collective-permute-start(bf16[8,2,64,128]{3,2,1,0:T(8,128)(2,1)S(1)} %collective-permute-done.10.refs_6_), channel_id=1, source_target_pairs={{0,7},{1,0},{2,1},{3,2},{4,3},{5,4},{6,5},{7,6},{8,15},{9,8},{10,9... | collective-permute-start | bytes 786440 | tf_op jit(solution)/shard_map/ppermute | solution.py:43
  45.2 1.1 %collective-permute-done.8.vp = bf16[256,128]{1,0:T(8,128)(2,1)S(1)} collective-permute-done((bf16[256,128]{1,0:T(8,128)(2,1)S(1)}, bf16[256,128]{1,0:T(8,128)(2,1)S(1)}, u32[]{:S(2)}, u32[]{:S(2)}) %collective-permute-start.8) | collective-permute-done | bytes 65568 | tf_op jit(solution)/shard_map/ppermute | solution.py:298
  46.4 0.9 copy-done.5
  47.3 2.2 %near.1 = (f32[4,256,128]{2,1,0:T(8,128)S(1)}, f32[4,256,128]{2,1,0:T(8,128)S(1)}, f32[4,256,128]{2,1,0:T(8,128)S(1)}) custom-call(s32[1,4]{1,0:T(1,128)S(1)} %copy-done.4, s32[1]{0:T(128)S(6)} %copy.14.cnt, bf16[256,512]{1,0:T(8,128)(2,1)S(1)} %copy-done.5, bf16[256,128]{1,0:T(8,128)(2,1)S(1)} %collective-permute-done.7.kp, ...), custom_call_target="tpu_custom_call" | custom-call | flops 2200000000 | tf_op jit(solution)/shard_map/near/pallas_call | solution.py:303
  49.5 1.3 %row.1 = (bf16[2,512,128]{2,1,0:T(8,128)(2,1)S(1)}, bf16[2,512,128]{2,1,0:T(8,128)(2,1)S(1)}) custom-call(s32[128]{0:T(128)S(1)} %compare_select_fusion.1.tab, bf16[8,2,64,128]{3,2,1,0:T(8,128)(2,1)S(1)} %column.1.refs_0_, bf16[8,2,64,128]{3,2,1,0:T(8,128)(2,1)S(1)} %collective-permute-done.3.refs_1_, ...), custom_call_target="tpu_custom_call" | custom-call | flops 1300000000 | tf_op jit(solution)/shard_map/row/pallas_call | solution.py:315
  50.9 0.4 collective-permute-start.17
  51.3 2.9 %collective-permute-start.14 = (bf16[2,512,128]{2,1,0:T(8,128)(2,1)S(1)}, bf16[2,512,128]{2,1,0:T(8,128)(2,1)S(1)}, u32[]{:S(2)}, u32[]{:S(2)}) collective-permute-start(bf16[2,512,128]{2,1,0:T(8,128)(2,1)S(1)} %get-tuple-element.54.hi), channel_id=1, source_target_pairs={{0,24},{1,25},{2,26},{3,27},{4,28},{5,29},{6,30},{7,31},{8,0},{9,1... | collective-permute-start | bytes 786440 | tf_op jit(solution)/shard_map/ppermute | solution.py:37
  54.2 3.2 %collective-permute-start.16 = (bf16[2,512,128]{2,1,0:T(8,128)(2,1)S(1)}, bf16[2,512,128]{2,1,0:T(8,128)(2,1)S(1)}, u32[]{:S(2)}, u32[]{:S(2)}) collective-permute-start(bf16[2,512,128]{2,1,0:T(8,128)(2,1)S(1)} %get-tuple-element.53.lo), channel_id=1, source_target_pairs={{0,24},{1,25},{2,26},{3,27},{4,28},{5,29},{6,30},{7,31},{8,0},{9,1... | collective-permute-start | bytes 786440 | tf_op jit(solution)/shard_map/ppermute | solution.py:37
  57.4 3.1 %far.3 = (f32[4,256,128]{2,1,0:T(8,128)S(1)}, f32[4,256,128]{2,1,0:T(8,128)S(1)}, f32[4,256,128]{2,1,0:T(8,128)S(1)}) custom-call(s32[128]{0:T(128)S(1)} %compare_select_fusion.1.tab, bf16[256,512]{1,0:T(8,128)(2,1)S(1)} %copy-done.6, bf16[2,512,128]{2,1,0:T(8,128)(2,1)S(1)} %get-tuple-element.53.lo, bf16[2,512,128]{2,1,0:T(8,128)(2,1)S(1)} %get-tuple-element.54.hi, ...), custom_call_target="tpu_custom_call" | custom-call | flops 2500000000 | tf_op jit(solution)/shard_map/far/pallas_call | solution.py:328
  60.6 3.7 %collective-permute-done.12.lo = bf16[2,512,128]{2,1,0:T(8,128)(2,1)S(1)} collective-permute-done((bf16[2,512,128]{2,1,0:T(8,128)(2,1)S(1)}, bf16[2,512,128]{2,1,0:T(8,128)(2,1)S(1)}, u32[]{:S(2)}, u32[]{:S(2)}) %collective-permute-start.12) | collective-permute-done | bytes 262176 | tf_op jit(solution)/shard_map/ppermute | solution.py:37
  64.3 3.2 %collective-permute-start.15 = (bf16[2,512,128]{2,1,0:T(8,128)(2,1)S(1)}, bf16[2,512,128]{2,1,0:T(8,128)(2,1)S(1)}, u32[]{:S(2)}, u32[]{:S(2)}) collective-permute-start(bf16[2,512,128]{2,1,0:T(8,128)(2,1)S(1)} %collective-permute-done.14.hi), channel_id=1, source_target_pairs={{0,24},{1,25},{2,26},{3,27},{4,28},{5,29},{6,30},{7,31},{8,0},{9,1... | collective-permute-start | bytes 786440 | tf_op jit(solution)/shard_map/ppermute | solution.py:37
  67.6 3.1 %far.4 = (f32[4,256,128]{2,1,0:T(8,128)S(1)}, f32[4,256,128]{2,1,0:T(8,128)S(1)}, f32[4,256,128]{2,1,0:T(8,128)S(1)}) custom-call(s32[128]{0:T(128)S(1)} %compare_select_fusion.1.tab, bf16[256,512]{1,0:T(8,128)(2,1)S(1)} %copy-done.6, bf16[2,512,128]{2,1,0:T(8,128)(2,1)S(1)} %collective-permute-done.12.lo, ...), custom_call_target="tpu_custom_call" | custom-call | flops 2500000000 | tf_op jit(solution)/shard_map/far/pallas_call | solution.py:328
  70.7 3.1 %far.5 = (f32[4,256,128]{2,1,0:T(8,128)S(1)}, f32[4,256,128]{2,1,0:T(8,128)S(1)}, f32[4,256,128]{2,1,0:T(8,128)S(1)}) custom-call(s32[128]{0:T(128)S(1)} %compare_select_fusion.1.tab, bf16[256,512]{1,0:T(8,128)(2,1)S(1)} %copy-done.6, bf16[2,512,128]{2,1,0:T(8,128)(2,1)S(1)} %collective-permute-done.16.lo, ...), custom_call_target="tpu_custom_call" | custom-call | flops 2500000000 | tf_op jit(solution)/shard_map/far/pallas_call | solution.py:328
  73.8 3.1 %last.1.att = bf16[256,512]{1,0:T(8,128)(2,1)S(1)} custom-call(s32[128]{0:T(128)S(1)} %compare_select_fusion.1.tab, bf16[256,512]{1,0:T(8,128)(2,1)S(1)} %copy-done.6, bf16[2,512,128]{2,1,0:T(8,128)(2,1)S(1)} %collective-permute-done.13.lo, bf16[2,512,128]{2,1,0:T(8,128)(2,1)S(1)} %collective-permute-done.15.hi, f32[4,256,128]{2,1,0:T(8,128)S(1)} %get-tuple-element.64.m_in, ...), custom_call_target="tpu_custom_call" | custom-call | flops 2500000000 | tf_op jit(solution)/shard_map/last/pallas_call | solution.py:337
  77.0 1.6 %away.2 = bf16[3,256,512]{2,1,0:T(8,128)(2,1)S(1)} custom-call(s32[4]{0:T(128)S(1)} %add_subtract_fusion.cols, bf16[256,512]{1,0:T(8,128)(2,1)S(1)} %last.1.att, bf16[512,4096]{1,0:T(8,128)(2,1)S(1)} %copy-done.1), custom_call_target="tpu_custom_call" | custom-call | flops 1500000000 | tf_op jit(solution)/shard_map/away/pallas_call | solution.py:365
  78.7 0.8 away.3
  79.6 0.6 collective-permute-start.19
  80.2 1.2 %collective-permute-done.19.recv = bf16[1,256,512]{2,1,0:T(8,128)(2,1)S(1)} collective-permute-done((bf16[1,256,512]{2,1,0:T(8,128)(2,1)S(1)}, bf16[1,256,512]{2,1,0:T(8,128)(2,1)S(1)}, u32[]{:S(2)}, u32[]{:S(2)}) %collective-permute-start.19) | collective-permute-done | bytes 262176 | tf_op jit(solution)/shard_map/ppermute | solution.py:55
  81.4 0.8 halves.1
  82.2 0.6 collective-permute-start.20
  82.8 1.5 %collective-permute-start.21 = (bf16[128,512]{1,0:T(8,128)(2,1)S(1)}, bf16[128,512]{1,0:T(8,128)(2,1)S(1)}, u32[]{:S(2)}, u32[]{:S(2)}) collective-permute-start(bf16[128,512]{1,0:T(8,128)(2,1)S(1)} %get-tuple-element.68), channel_id=1, source_target_pairs={{0,192},{32,224},{64,0},{96,32},{128,64},{160,96},{192,128},{224,1... | collective-permute-start | bytes 393224 | tf_op jit(solution)/shard_map/ppermute | solution.py:49
  84.3 1.6 %home.1 = f32[3,256,512]{2,1,0:T(8,128)S(1)} custom-call(s32[4]{0:T(128)S(1)} %broadcast_add_fusion.cols, bf16[256,512]{1,0:T(8,128)(2,1)S(1)} %last.1.att, bf16[512,4096]{1,0:T(8,128)(2,1)S(1)} %copy-done.1, bf16[3,256,512]{2,1,0:T(8,128)(2,1)S(1)} %collective-permute-done.18.recv), custom_call_target="tpu_custom_call" | custom-call | flops 1500000000 | tf_op jit(solution)/shard_map/home/pallas_call | solution.py:395
  86.0 2.0 %collective-permute-done.20.a = bf16[128,512]{1,0:T(8,128)(2,1)S(1)} collective-permute-done((bf16[128,512]{1,0:T(8,128)(2,1)S(1)}, bf16[128,512]{1,0:T(8,128)(2,1)S(1)}, u32[]{:S(2)}, u32[]{:S(2)}) %collective-permute-start.20) | collective-permute-done | bytes 131104 | tf_op jit(solution)/shard_map/ppermute | solution.py:49
  88.0 1.4 %collective-permute-done.21.b = bf16[128,512]{1,0:T(8,128)(2,1)S(1)} collective-permute-done((bf16[128,512]{1,0:T(8,128)(2,1)S(1)}, bf16[128,512]{1,0:T(8,128)(2,1)S(1)}, u32[]{:S(2)}, u32[]{:S(2)}) %collective-permute-start.21) | collective-permute-done | bytes 131104 | tf_op jit(solution)/shard_map/ppermute | solution.py:49
  89.5 0.4 collective-permute-start.22
  89.9 1.7 %collective-permute-start.23 = (bf16[256,512]{1,0:T(8,128)(2,1)S(1)}, bf16[256,512]{1,0:T(8,128)(2,1)S(1)}, u32[]{:S(2)}, u32[]{:S(2)}) collective-permute-start(bf16[256,512]{1,0:T(8,128)(2,1)S(1)} %get-tuple-element.70), channel_id=1, source_target_pairs={{0,192},{32,224},{64,0},{96,32},{128,64},{160,96},{192,128},{224,1... | collective-permute-start | bytes 786440 | tf_op jit(solution)/shard_map/ppermute | solution.py:49
  91.6 5.4 %collective-permute-done.22.a = bf16[256,512]{1,0:T(8,128)(2,1)S(1)} collective-permute-done((bf16[256,512]{1,0:T(8,128)(2,1)S(1)}, bf16[256,512]{1,0:T(8,128)(2,1)S(1)}, u32[]{:S(2)}, u32[]{:S(2)}) %collective-permute-start.22) | collective-permute-done | bytes 262176 | tf_op jit(solution)/shard_map/ppermute | solution.py:49
  97.0 1.5 %collective-permute-done.23.b = bf16[256,512]{1,0:T(8,128)(2,1)S(1)} collective-permute-done((bf16[256,512]{1,0:T(8,128)(2,1)S(1)}, bf16[256,512]{1,0:T(8,128)(2,1)S(1)}, u32[]{:S(2)}, u32[]{:S(2)}) %collective-permute-start.23) | collective-permute-done | bytes 262176 | tf_op jit(solution)/shard_map/ppermute | solution.py:49
  98.5 0.8 final.1
  (50 shorter events, 0.6 us)
Async XLA Ops:
  0.0 20.4 %copy-start = (bf16[4096,128]{1,0:T(8,128)(2,1)S(1)}, bf16[4096,128]{1,0:T(8,128)(2,1)}, u32[]{:S(2)}) copy-start(bf16[4096,128]{1,0:T(8,128)(2,1)} %param.16) | copy-start | bytes 3145732
  1.7 1.0 copy-start.2
  2.7 0.9 copy-start.3
  3.6 5.9 %copy-start.7 = (bf16[256,4096]{1,0:T(8,128)(2,1)S(1)}, bf16[256,4096]{1,0:T(8,128)(2,1)}, u32[]{:S(2)}) copy-start(bf16[256,4096]{1,0:T(8,128)(2,1)} %param.12) | copy-start | bytes 6291460
  3.6 6.4 %copy-start.9 = (f32[4096]{0:T(1024)S(1)}, f32[4096]{0:T(1024)}, u32[]{:S(2)}) copy-start(f32[4096]{0:T(1024)} %param.13) | copy-start | bytes 49156
  4.2 6.5 %collective-permute-start.2 = (bf16[2,2,64,128]{3,2,1,0:T(8,128)(2,1)S(1)}, bf16[2,2,64,128]{3,2,1,0:T(8,128)(2,1)S(1)}, u32[]{:S(2)}, u32[]{:S(2)}) collective-permute-start(bf16[2,2,64,128]{3,2,1,0:T(8,128)(2,1)S(1)} %get-tuple-element.41), channel_id=1, source_target_pairs={{0,24},{1,25},{2,26},{3,27},{4,28},{5,29},{6,30},{7,31},{8,0},{9,1... | collective-permute-start | bytes 196616 | tf_op jit(solution)/shard_map/ppermute | solution.py:37
  7.3 6.3 %collective-permute-start = (bf16[2,2,64,128]{3,2,1,0:T(8,128)(2,1)S(1)}, bf16[2,2,64,128]{3,2,1,0:T(8,128)(2,1)S(1)}, u32[]{:S(2)}, u32[]{:S(2)}) collective-permute-start(bf16[2,2,64,128]{3,2,1,0:T(8,128)(2,1)S(1)} %get-tuple-element.39), channel_id=1, source_target_pairs={{0,8},{1,9},{2,10},{3,11},{4,12},{5,13},{6,14},{7,15},{8,16},{9,17... | collective-permute-start | bytes 196616 | tf_op jit(solution)/shard_map/ppermute | solution.py:37
  7.3 6.3 %collective-permute-start.1 = (bf16[2,2,64,128]{3,2,1,0:T(8,128)(2,1)S(1)}, bf16[2,2,64,128]{3,2,1,0:T(8,128)(2,1)S(1)}, u32[]{:S(2)}, u32[]{:S(2)}) collective-permute-start(bf16[2,2,64,128]{3,2,1,0:T(8,128)(2,1)S(1)} %get-tuple-element.40), channel_id=1, source_target_pairs={{0,16},{1,17},{2,18},{3,19},{4,20},{5,21},{6,22},{7,23},{8,24},{9,... | collective-permute-start | bytes 196616 | tf_op jit(solution)/shard_map/ppermute | solution.py:37
  14.4 6.8 %copy-start.8 = (bf16[4096,128]{1,0:T(8,128)(2,1)S(1)}, bf16[4096,128]{1,0:T(8,128)(2,1)}, u32[]{:S(2)}) copy-start(bf16[4096,128]{1,0:T(8,128)(2,1)} %param.15) | copy-start | bytes 3145732
  14.4 10.9 %collective-permute-start.3 = (bf16[8,2,64,128]{3,2,1,0:T(8,128)(2,1)S(1)}, bf16[8,2,64,128]{3,2,1,0:T(8,128)(2,1)S(1)}, u32[]{:S(2)}, u32[]{:S(2)}) collective-permute-start(bf16[8,2,64,128]{3,2,1,0:T(8,128)(2,1)S(1)} %column.1.refs_0_), channel_id=1, source_target_pairs={{0,1},{1,2},{2,3},{3,4},{4,5},{5,6},{6,7},{7,0},{8,9},{9,10},{10,1... | collective-permute-start | bytes 786440 | tf_op jit(solution)/shard_map/ppermute | solution.py:43
  16.4 16.5 %collective-permute-start.9 = (bf16[8,2,64,128]{3,2,1,0:T(8,128)(2,1)S(1)}, bf16[8,2,64,128]{3,2,1,0:T(8,128)(2,1)S(1)}, u32[]{:S(2)}, u32[]{:S(2)}) collective-permute-start(bf16[8,2,64,128]{3,2,1,0:T(8,128)(2,1)S(1)} %column.1.refs_0_), channel_id=1, source_target_pairs={{0,7},{1,0},{2,1},{3,2},{4,3},{5,4},{6,5},{7,6},{8,15},{9,8},{10,9... | collective-permute-start | bytes 786440 | tf_op jit(solution)/shard_map/ppermute | solution.py:43
  20.4 4.9 %copy-start.10 = (bf16[4096,512]{1,0:T(8,128)(2,1)S(1)}, bf16[4096,512]{1,0:T(8,128)(2,1)}, u32[]{:S(2)}) copy-start(bf16[4096,512]{1,0:T(8,128)(2,1)} %param.14) | copy-start | bytes 12582916
  21.9 24.5 %copy-start.4 = (s32[1,4]{1,0:T(1,128)S(1)}, s32[1,4]{1,0:T(1,128)}, u32[]{:S(2)}) copy-start(s32[1,4]{1,0:T(1,128)} %offs.1) | copy-start | bytes 52
  25.3 7.6 %collective-permute-start.4 = (bf16[8,2,64,128]{3,2,1,0:T(8,128)(2,1)S(1)}, bf16[8,2,64,128]{3,2,1,0:T(8,128)(2,1)S(1)}, u32[]{:S(2)}, u32[]{:S(2)}) collective-permute-start(bf16[8,2,64,128]{3,2,1,0:T(8,128)(2,1)S(1)} %collective-permute-done.3.refs_1_), channel_id=1, source_target_pairs={{0,1},{1,2},{2,3},{3,4},{4,5},{5,6},{6,7},{7,0},{8,9},{9,10},{10,1... | collective-permute-start | bytes 786440 | tf_op jit(solution)/shard_map/ppermute | solution.py:43
  32.9 8.1 %collective-permute-start.5 = (bf16[8,2,64,128]{3,2,1,0:T(8,128)(2,1)S(1)}, bf16[8,2,64,128]{3,2,1,0:T(8,128)(2,1)S(1)}, u32[]{:S(2)}, u32[]{:S(2)}) collective-permute-start(bf16[8,2,64,128]{3,2,1,0:T(8,128)(2,1)S(1)} %collective-permute-done.4.refs_2_), channel_id=1, source_target_pairs={{0,1},{1,2},{2,3},{3,4},{4,5},{5,6},{6,7},{7,0},{8,9},{9,10},{10,1... | collective-permute-start | bytes 786440 | tf_op jit(solution)/shard_map/ppermute | solution.py:43
  32.9 8.1 %collective-permute-start.10 = (bf16[8,2,64,128]{3,2,1,0:T(8,128)(2,1)S(1)}, bf16[8,2,64,128]{3,2,1,0:T(8,128)(2,1)S(1)}, u32[]{:S(2)}, u32[]{:S(2)}) collective-permute-start(bf16[8,2,64,128]{3,2,1,0:T(8,128)(2,1)S(1)} %collective-permute-done.9.refs_7_), channel_id=1, source_target_pairs={{0,7},{1,0},{2,1},{3,2},{4,3},{5,4},{6,5},{7,6},{8,15},{9,8},{10,9... | collective-permute-start | bytes 786440 | tf_op jit(solution)/shard_map/ppermute | solution.py:43
  36.2 9.1 %collective-permute-start.7 = (bf16[256,128]{1,0:T(8,128)(2,1)S(1)}, bf16[256,128]{1,0:T(8,128)(2,1)S(1)}, u32[]{:S(2)}, u32[]{:S(2)}) collective-permute-start(bf16[256,128]{1,0:T(8,128)(2,1)S(1)} %convolution_convert_fusion.2.k), channel_id=1, source_target_pairs={{0,1},{1,2},{2,3},{3,4},{4,5},{5,6},{6,7},{7,8},{8,9},{9,10},{10,1... | collective-permute-start | bytes 196616 | tf_op jit(solution)/shard_map/ppermute | solution.py:298
  36.2 10.2 %collective-permute-start.8 = (bf16[256,128]{1,0:T(8,128)(2,1)S(1)}, bf16[256,128]{1,0:T(8,128)(2,1)S(1)}, u32[]{:S(2)}, u32[]{:S(2)}) collective-permute-start(bf16[256,128]{1,0:T(8,128)(2,1)S(1)} %convolution_convert_fusion.1.v), channel_id=1, source_target_pairs={{0,1},{1,2},{2,3},{3,4},{4,5},{5,6},{6,7},{7,8},{8,9},{9,10},{10,1... | collective-permute-start | bytes 196616 | tf_op jit(solution)/shard_map/ppermute | solution.py:298
  41.1 8.4 %collective-permute-start.6 = (bf16[8,2,64,128]{3,2,1,0:T(8,128)(2,1)S(1)}, bf16[8,2,64,128]{3,2,1,0:T(8,128)(2,1)S(1)}, u32[]{:S(2)}, u32[]{:S(2)}) collective-permute-start(bf16[8,2,64,128]{3,2,1,0:T(8,128)(2,1)S(1)} %collective-permute-done.5.refs_3_), channel_id=1, source_target_pairs={{0,1},{1,2},{2,3},{3,4},{4,5},{5,6},{6,7},{7,0},{8,9},{9,10},{10,1... | collective-permute-start | bytes 786440 | tf_op jit(solution)/shard_map/ppermute | solution.py:43
  41.1 8.5 %collective-permute-start.11 = (bf16[8,2,64,128]{3,2,1,0:T(8,128)(2,1)S(1)}, bf16[8,2,64,128]{3,2,1,0:T(8,128)(2,1)S(1)}, u32[]{:S(2)}, u32[]{:S(2)}) collective-permute-start(bf16[8,2,64,128]{3,2,1,0:T(8,128)(2,1)S(1)} %collective-permute-done.10.refs_6_), channel_id=1, source_target_pairs={{0,7},{1,0},{2,1},{3,2},{4,3},{5,4},{6,5},{7,6},{8,15},{9,8},{10,9... | collective-permute-start | bytes 786440 | tf_op jit(solution)/shard_map/ppermute | solution.py:43
  46.4 1.0 copy-start.5
  49.5 7.9 %copy-start.6 = (bf16[256,512]{1,0:T(8,128)(2,1)S(1)}, bf16[256,512]{1,0:T(8,128)(2,1)}, u32[]{:S(2)}) copy-start(bf16[256,512]{1,0:T(8,128)(2,1)} %convolution_convert_fusion.q) | copy-start | bytes 786436
  50.9 16.7 %collective-permute-start.17 = (bf16[2,512,128]{2,1,0:T(8,128)(2,1)S(1)}, bf16[2,512,128]{2,1,0:T(8,128)(2,1)S(1)}, u32[]{:S(2)}, u32[]{:S(2)}) collective-permute-start(bf16[2,512,128]{2,1,0:T(8,128)(2,1)S(1)} %get-tuple-element.54.hi), channel_id=1, source_target_pairs={{0,8},{1,9},{2,10},{3,11},{4,12},{5,13},{6,14},{7,15},{8,16},{9,17... | collective-permute-start | bytes 786440 | tf_op jit(solution)/shard_map/ppermute | solution.py:37
  51.3 13.0 %collective-permute-start.14 = (bf16[2,512,128]{2,1,0:T(8,128)(2,1)S(1)}, bf16[2,512,128]{2,1,0:T(8,128)(2,1)S(1)}, u32[]{:S(2)}, u32[]{:S(2)}) collective-permute-start(bf16[2,512,128]{2,1,0:T(8,128)(2,1)S(1)} %get-tuple-element.54.hi), channel_id=1, source_target_pairs={{0,24},{1,25},{2,26},{3,27},{4,28},{5,29},{6,30},{7,31},{8,0},{9,1... | collective-permute-start | bytes 786440 | tf_op jit(solution)/shard_map/ppermute | solution.py:37
  54.2 10.1 %collective-permute-start.12 = (bf16[2,512,128]{2,1,0:T(8,128)(2,1)S(1)}, bf16[2,512,128]{2,1,0:T(8,128)(2,1)S(1)}, u32[]{:S(2)}, u32[]{:S(2)}) collective-permute-start(bf16[2,512,128]{2,1,0:T(8,128)(2,1)S(1)} %get-tuple-element.53.lo), channel_id=1, source_target_pairs={{0,8},{1,9},{2,10},{3,11},{4,12},{5,13},{6,14},{7,15},{8,16},{9,17... | collective-permute-start | bytes 786440 | tf_op jit(solution)/shard_map/ppermute | solution.py:37
  54.2 16.5 %collective-permute-start.16 = (bf16[2,512,128]{2,1,0:T(8,128)(2,1)S(1)}, bf16[2,512,128]{2,1,0:T(8,128)(2,1)S(1)}, u32[]{:S(2)}, u32[]{:S(2)}) collective-permute-start(bf16[2,512,128]{2,1,0:T(8,128)(2,1)S(1)} %get-tuple-element.53.lo), channel_id=1, source_target_pairs={{0,24},{1,25},{2,26},{3,27},{4,28},{5,29},{6,30},{7,31},{8,0},{9,1... | collective-permute-start | bytes 786440 | tf_op jit(solution)/shard_map/ppermute | solution.py:37
  64.3 9.5 %collective-permute-start.13 = (bf16[2,512,128]{2,1,0:T(8,128)(2,1)S(1)}, bf16[2,512,128]{2,1,0:T(8,128)(2,1)S(1)}, u32[]{:S(2)}, u32[]{:S(2)}) collective-permute-start(bf16[2,512,128]{2,1,0:T(8,128)(2,1)S(1)} %collective-permute-done.12.lo), channel_id=1, source_target_pairs={{0,8},{1,9},{2,10},{3,11},{4,12},{5,13},{6,14},{7,15},{8,16},{9,17... | collective-permute-start | bytes 786440 | tf_op jit(solution)/shard_map/ppermute | solution.py:37
  64.3 9.5 %collective-permute-start.15 = (bf16[2,512,128]{2,1,0:T(8,128)(2,1)S(1)}, bf16[2,512,128]{2,1,0:T(8,128)(2,1)S(1)}, u32[]{:S(2)}, u32[]{:S(2)}) collective-permute-start(bf16[2,512,128]{2,1,0:T(8,128)(2,1)S(1)} %collective-permute-done.14.hi), channel_id=1, source_target_pairs={{0,24},{1,25},{2,26},{3,27},{4,28},{5,29},{6,30},{7,31},{8,0},{9,1... | collective-permute-start | bytes 786440 | tf_op jit(solution)/shard_map/ppermute | solution.py:37
  73.8 3.1 %copy-start.1 = (bf16[512,4096]{1,0:T(8,128)(2,1)S(1)}, bf16[512,4096]{1,0:T(8,128)(2,1)}, u32[]{:S(2)}) copy-start(bf16[512,4096]{1,0:T(8,128)(2,1)} %w.7) | copy-start | bytes 12582916
  78.6 5.7 %collective-permute-start.18 = (bf16[3,256,512]{2,1,0:T(8,128)(2,1)S(1)}, bf16[3,256,512]{2,1,0:T(8,128)(2,1)S(1)}, u32[]{:S(2)}, u32[]{:S(2)}) collective-permute-start(bf16[3,256,512]{2,1,0:T(8,128)(2,1)S(1)} %away.2), channel_id=1, source_target_pairs={{0,32},{32,0},{64,96},{96,64},{128,160},{160,128},{192,224},{224,1... | collective-permute-start | bytes 2359304 | tf_op jit(solution)/shard_map/ppermute | solution.py:55
  79.6 1.8 %collective-permute-start.19 = (bf16[1,256,512]{2,1,0:T(8,128)(2,1)S(1)}, bf16[1,256,512]{2,1,0:T(8,128)(2,1)S(1)}, u32[]{:S(2)}, u32[]{:S(2)}) collective-permute-start(bf16[1,256,512]{2,1,0:T(8,128)(2,1)S(1)} %away.3), channel_id=1, source_target_pairs={{0,32},{32,0},{64,96},{96,64},{128,160},{160,128},{192,224},{224,1... | collective-permute-start | bytes 786440 | tf_op jit(solution)/shard_map/ppermute | solution.py:55
  82.2 5.8 %collective-permute-start.20 = (bf16[128,512]{1,0:T(8,128)(2,1)S(1)}, bf16[128,512]{1,0:T(8,128)(2,1)S(1)}, u32[]{:S(2)}, u32[]{:S(2)}) collective-permute-start(bf16[128,512]{1,0:T(8,128)(2,1)S(1)} %get-tuple-element.67), channel_id=1, source_target_pairs={{0,64},{32,96},{64,128},{96,160},{128,192},{160,224},{192,0},{224,... | collective-permute-start | bytes 393224 | tf_op jit(solution)/shard_map/ppermute | solution.py:49
  82.8 6.7 %collective-permute-start.21 = (bf16[128,512]{1,0:T(8,128)(2,1)S(1)}, bf16[128,512]{1,0:T(8,128)(2,1)S(1)}, u32[]{:S(2)}, u32[]{:S(2)}) collective-permute-start(bf16[128,512]{1,0:T(8,128)(2,1)S(1)} %get-tuple-element.68), channel_id=1, source_target_pairs={{0,192},{32,224},{64,0},{96,32},{128,64},{160,96},{192,128},{224,1... | collective-permute-start | bytes 393224 | tf_op jit(solution)/shard_map/ppermute | solution.py:49
  89.5 7.5 %collective-permute-start.22 = (bf16[256,512]{1,0:T(8,128)(2,1)S(1)}, bf16[256,512]{1,0:T(8,128)(2,1)S(1)}, u32[]{:S(2)}, u32[]{:S(2)}) collective-permute-start(bf16[256,512]{1,0:T(8,128)(2,1)S(1)} %get-tuple-element.69), channel_id=1, source_target_pairs={{0,64},{32,96},{64,128},{96,160},{128,192},{160,224},{192,0},{224,... | collective-permute-start | bytes 786440 | tf_op jit(solution)/shard_map/ppermute | solution.py:49
  89.9 8.7 %collective-permute-start.23 = (bf16[256,512]{1,0:T(8,128)(2,1)S(1)}, bf16[256,512]{1,0:T(8,128)(2,1)S(1)}, u32[]{:S(2)}, u32[]{:S(2)}) collective-permute-start(bf16[256,512]{1,0:T(8,128)(2,1)S(1)} %get-tuple-element.70), channel_id=1, source_target_pairs={{0,192},{32,224},{64,0},{96,32},{128,64},{160,96},{192,128},{224,1... | collective-permute-start | bytes 786440 | tf_op jit(solution)/shard_map/ppermute | solution.py:49

commit v3 on v2

v3 whole, which is shorter than its diff:
```python
import functools
import math

import jax
import jax.numpy as jnp
from jax import lax
from jax.experimental import pallas as pl
from jax.experimental.pallas import tpu as pltpu
from jax.sharding import PartitionSpec as P

BLK = 64
HD = 128
GROUP = 4
NY = 4
NZ = 8
NX = 4
VMEM = pltpu.VMEM
VSPEC = pl.BlockSpec(memory_space=pltpu.VMEM)
HSPEC = pl.BlockSpec(memory_space=pltpu.HBM)
SSPEC = pl.BlockSpec(memory_space=pltpu.SMEM)
SCALE2 = math.log2(math.e) / math.sqrt(HD)
NEG = -jnp.inf


def params(mib):
    return pltpu.CompilerParams(vmem_limit_bytes=mib << 20)


def cost(us):
    return pl.CostEstimate(flops=int(us * 1e9), bytes_accessed=0, transcendentals=0)


def tie(*values):
    return lax.optimization_barrier(values)


def shift_y(block, d):
    return lax.ppermute(
        block, "seq", [(y * NZ + z, (y + d) % NY * NZ + z) for y in range(NY) for z in range(NZ)]
    )


def shift_z(block, d):
    return lax.ppermute(
        block, "seq", [(y * NZ + z, y * NZ + (z + d) % NZ) for y in range(NY) for z in range(NZ)]
    )


def shift_x(block, d):
    return lax.ppermute(
        block, "heads", [(2 * x + c, 2 * ((x + d) % NX) + c) for x in range(NX) for c in range(2)]
    )


def swap_core(block):
    return lax.ppermute(block, "heads", [(i, i ^ 1) for i in range(2 * NX)])


def position():
    me = lax.axis_index("seq")
    return me // NZ, lax.rem(me, NZ)


def at(tab, group):
    return tab[64 + group]


def pick_kernel(tab, ck, cv, *refs):
    outs, sems = refs[:NY], refs[NY]
    y, z = position()
    group = z * NY + y
    start = at(tab, group)
    size = at(tab, group + 1) - start
    copies = []
    for dy in range(NY):
        for j in range(2):
            i = ((y + dy - start) & 3) + 4 * j
            entry = tab[jnp.minimum(start + i, 63)]
            row = pl.multiple_of(jnp.where(i < size, entry & 15, 0) * BLK, BLK)
            for k, cache in enumerate((ck, cv)):
                copies.append(
                    pltpu.make_async_copy(
                        cache.at[0, pl.ds(row, BLK)], outs[dy].at[j, k], sems.at[len(copies)]
                    )
                )
    for copy in copies:
        copy.start()
    for copy in copies:
        copy.wait()


def column_kernel(tab, r0, r1, r2, r3, out):
    y, z = position()
    recv = (r0, r1, r2, r3)
    start = at(tab, z * NY)
    size = at(tab, z * NY + NY) - start
    first = (y - start) & 3
    for i in range(8):
        off = first + 4 * i
        live = off < size
        r = jnp.minimum(start + off, 63)
        hy = (tab[r] >> 4) & 3
        j = jnp.where(live, (r - at(tab, z * NY + hy)) >> 2, 0)
        d = jnp.where(live, (y - hy) & 3, 0)
        for k in range(NY):

            @pl.when(d == k)
            def _():
                out[i] = recv[k][j]


def row_kernel(tab, *refs):
    y, z = position()
    recv, outs = refs[:NZ], refs[NZ:]
    for m in range(16):
        r = y + 4 * m
        live = r < at(tab, 32)
        zs = jnp.where(live, tab[r] >> 6, z)
        start = at(tab, zs * NY)
        first = (y - start) & 3
        i = jnp.where(live, (r - start - first) >> 2, 0)
        d = (z - zs) & 7
        out, place = outs[m // 8], m % 8 * BLK
        for k in range(NZ):

            @pl.when(d == k)
            def _():
                out[0, place : place + BLK] = recv[k][i, 0]
                out[1, place : place + BLK] = recv[k][i, 1]


def near_kernel(offs, cnt, q, kp, vp, k, v, m_out, l_out, acc_out):
    me = lax.axis_index("seq")
    rows = k.shape[0]
    keys = jnp.concatenate([kp[...], k[...]], axis=0)
    values = jnp.concatenate([vp[...], v[...]], axis=0)
    t = lax.broadcasted_iota(jnp.int32, (rows, 2 * rows), 0)
    u = lax.broadcasted_iota(jnp.int32, (rows, 2 * rows), 1) - rows
    gap = (t >> 6) - (u >> 6)
    hit = (gap == 0) & (u <= t)
    for e in range(4):
        off = jnp.where((e < cnt[0]) & (offs[0, e] >= 0), offs[0, e], -100)
        hit = hit | (gap == off)
    hit = hit & (u >= jnp.where(me > 0, -rows, 0))
    for h in range(GROUP):
        s = lax.dot_general(
            q[:, h * HD : (h + 1) * HD],
            keys,
            (((1,), (1,)), ((), ())),
            preferred_element_type=jnp.float32,
        )
        s = jnp.where(hit, s, NEG)
        top = jnp.broadcast_to(jnp.max(s, axis=1, keepdims=True), (rows, HD))
        p = jnp.exp2((s - across(top, 2 * rows)) * SCALE2)
        m_out[h] = top
        l_out[h] = lane_sums(p)
        acc_out[h] = jnp.dot(p.astype(jnp.bfloat16), values, preferred_element_type=jnp.float32)


def across(x, width):
    return jnp.concatenate([x] * (width // HD), axis=1)


def lane_sums(p):
    total = p[:, :HD]
    for i in range(HD, p.shape[1], HD):
        total = total + p[:, i : i + HD]
    return total


def scores_of(q, h, k):
    return lax.dot_general(
        q[:, h * HD : (h + 1) * HD], k, (((1,), (1,)), ((), ())), preferred_element_type=jnp.float32
    )


def across(x, width):
    return jnp.concatenate([x] * (width // HD), axis=1)


def lane_sums(p):
    total = p[:, :HD]
    for i in range(HD, p.shape[1], HD):
        total = total + p[:, i : i + HD]
    return total


def scores_of(q, h, k):
    return lax.dot_general(
        q[:, h * HD : (h + 1) * HD], k, (((1,), (1,)), ((), ())), preferred_element_type=jnp.float32
    )


def update(scores, values, live, old, total, acc):
    masked, base = [], 0
    for s in scores:
        key = base + lax.broadcasted_iota(jnp.int32, s.shape, 1)
        masked.append(jnp.where(key < live, s, NEG))
        base += s.shape[1]
    top = functools.reduce(jnp.maximum, [jnp.max(s, axis=1, keepdims=True) for s in masked])
    top = jnp.maximum(old, jnp.broadcast_to(top, old.shape))
    factor = jnp.exp2((old - top) * SCALE2)
    total, acc = total * factor, acc * factor
    for s, v in zip(masked, values):
        p = jnp.exp2((s - across(top, s.shape[1])) * SCALE2)
        total = total + lane_sums(p)
        acc = acc + jnp.dot(p.astype(jnp.bfloat16), v, preferred_element_type=jnp.float32)
    return top, total, acc


def row_sum(total):
    return jnp.broadcast_to(jnp.sum(total, axis=1, keepdims=True), total.shape)


def each_head(tab, shift, q, lo, hi, m_in, l_in, acc_in):
    y, _ = position()
    live = ((at(tab, 32) - ((y - shift) & 3) + 3) >> 2) * BLK
    following = [scores_of(q, 0, lo[0]), scores_of(q, 0, hi[0])]
    for h in range(GROUP):
        current = following
        if h + 1 < GROUP:
            following = [scores_of(q, h + 1, lo[0]), scores_of(q, h + 1, hi[0])]
        yield h, update(current, (lo[1], hi[1]), live, m_in[h], l_in[h], acc_in[h])


def far_kernel(shift, tab, q, lo, hi, m_in, l_in, acc_in, m_out, l_out, acc_out):
    for h, new in each_head(tab, shift, q, lo, hi, m_in, l_in, acc_in):
        m_out[h], l_out[h], acc_out[h] = new


def last_kernel(shift, tab, q, lo, hi, m_in, l_in, acc_in, att):
    for h, (_, total, acc) in each_head(tab, shift, q, lo, hi, m_in, l_in, acc_in):
        att[:, h * HD : (h + 1) * HD] = (acc / row_sum(total)).astype(jnp.bfloat16)


def product_kernel(cols, att, w, out):
    out[0] = jnp.dot(att[...], w[...], preferred_element_type=jnp.float32).astype(out.dtype)


def halves_kernel(mine, recv, a, b):
    total = (mine[2] + recv[2].astype(jnp.float32)).astype(a.dtype)
    half = a.shape[0]
    a[...] = total[:half]
    b[...] = total[half:]


def pass_kernel(mine, recv, a, b, right, left):
    half = a.shape[0]
    forth = mine[1] + recv[1].astype(jnp.float32)
    back = mine[3] + recv[3].astype(jnp.float32)
    right[:half] = (forth[:half] + a[...].astype(jnp.float32)).astype(right.dtype)
    right[half:] = forth[half:].astype(right.dtype)
    left[:half] = back[:half].astype(left.dtype)
    left[half:] = (back[half:] + b[...].astype(jnp.float32)).astype(left.dtype)


def final_kernel(mine, recv, a, b, out):
    total = mine[0] + recv[0].astype(jnp.float32)
    total = total + a[...].astype(jnp.float32) + b[...].astype(jnp.float32)
    out[...] = total.astype(out.dtype)


def local(
    tokens,
    norm_gain,
    w_query,
    w_key,
    w_value,
    w_out,
    cache_keys,
    cache_values,
    vert_blocks,
    vert_count,
    slash_offsets,
    slash_count,
):
    rows = tokens.shape[0]
    bf16 = jnp.bfloat16
    f32 = jnp.float32
    blocks = vert_blocks[0]
    index = jnp.arange(128, dtype=jnp.int32)
    entry = index[:64]
    key = jnp.where(
        entry < vert_count[0],
        (((blocks >> 4) & 7) << 6) | ((blocks >> 7) << 4) | (blocks & 15),
        4096 + entry,
    )
    edges = jnp.concatenate([key, entry * 16])
    below = jnp.sum((key[None, :] < edges[:, None]).astype(jnp.int32), axis=1)
    ranked = jnp.sum(jnp.where(below[None, :64] == index[:, None], key[None, :], 0), axis=1)
    tab = jnp.where(index < 64, ranked, below)
    heads = lax.axis_index("heads")
    x, core = heads // 2, lax.rem(heads, 2)
    order = ((x + entry[:NX]) & 3) * 2
    tab, away_cols, home_cols = tie(tab, order + 1 - core, order + core)

    slot = jax.ShapeDtypeStruct((2, 2, BLK, HD), bf16)
    picked = pl.pallas_call(
        pick_kernel,
        out_shape=[slot] * NY,
        in_specs=[SSPEC, HSPEC, HSPEC],
        out_specs=[VSPEC] * NY,
        scratch_shapes=[pltpu.SemaphoreType.DMA((16,))],
        compiler_params=params(60),
        cost_estimate=cost(0.7),
        name="pick",
    )(tab, cache_keys, cache_values)
    spread = [picked[0]] + [shift_y(picked[d], d) for d in range(1, NY)]
    activation = tokens.astype(f32)
    normed = (
        activation
        * lax.rsqrt(jnp.mean(activation * activation, axis=-1, keepdims=True) + 1e-05)
        * norm_gain
    ).astype(bf16)
    spread[3], normed = tie(spread[3], normed)
    column = pl.pallas_call(
        column_kernel,
        out_shape=jax.ShapeDtypeStruct((8, 2, BLK, HD), bf16),
        in_specs=[SSPEC] + [VSPEC] * NY,
        out_specs=VSPEC,
        compiler_params=params(8),
        cost_estimate=cost(0.8),
        name="column",
    )(tab, *spread)
    key_rows = jnp.dot(normed, w_key, preferred_element_type=f32).astype(bf16)
    value_rows = jnp.dot(normed, w_value, preferred_element_type=f32).astype(bf16)
    seqs = lax.axis_size("seq")
    route = [(i, (i + 1) % seqs) for i in range(seqs)]
    ring = [column] + [None] * 7
    ring[1], ring[7] = shift_z(column, 1), shift_z(column, -1)
    ring[1], key_rows, value_rows = tie(ring[1], key_rows, value_rows)
    ring[2], ring[6] = shift_z(ring[1], 1), shift_z(ring[7], -1)
    before_keys, before_values = lax.ppermute((key_rows, value_rows), "seq", route)
    queries = jnp.dot(normed, w_query, preferred_element_type=f32).astype(bf16)
    ring[2], queries = tie(ring[2], queries)
    ring[3], ring[5] = shift_z(ring[2], 1), shift_z(ring[6], -1)
    state_shape = [jax.ShapeDtypeStruct((GROUP, rows, HD), f32)] * 3
    state = pl.pallas_call(
        near_kernel,
        out_shape=state_shape,
        in_specs=[SSPEC] * 2 + [VSPEC] * 5,
        out_specs=[VSPEC] * 3,
        compiler_params=params(16),
        cost_estimate=cost(2.2),
        name="near",
    )(slash_offsets, slash_count, queries, before_keys, before_values, key_rows, value_rows)
    ring[4] = shift_z(ring[3], 1)
    ring[4], *state = tie(ring[4], *state)
    half = jax.ShapeDtypeStruct((2, 8 * BLK, HD), bf16)
    own = pl.pallas_call(
        row_kernel,
        out_shape=[half] * 2,
        in_specs=[SSPEC] + [VSPEC] * NZ,
        out_specs=[VSPEC] * 2,
        compiler_params=params(16),
        cost_estimate=cost(1.3),
        name="row",
    )(tab, *ring)
    def far(shift, part, state):
        return pl.pallas_call(
            functools.partial(far_kernel, shift),
            out_shape=state_shape,
            in_specs=[SSPEC] + [VSPEC] * 6,
            out_specs=[VSPEC] * 3,
            compiler_params=params(16),
            cost_estimate=cost(1.8),
            name="far",
        )(tab, queries, *part, *state)

    lo1, hi3 = shift_y(own[0], 1), shift_y(own[1], -1)
    own_lo, own_hi, *state = tie(*own, *far(0, own, state))
    hi1, lo3 = shift_y(own_hi, 1), shift_y(own_lo, -1)
    lo2, hi2 = shift_y(lo1, 1), shift_y(hi3, -1)
    state = far(1, (lo1, hi1), state)
    state = far(3, (lo3, hi3), state)
    attended = pl.pallas_call(
        functools.partial(last_kernel, 2),
        out_shape=jax.ShapeDtypeStruct((rows, GROUP * HD), bf16),
        in_specs=[SSPEC] + [VSPEC] * 6,
        out_specs=VSPEC,
        compiler_params=params(16),
        cost_estimate=cost(2.5),
        name="last",
    )(tab, queries, lo2, hi2, *state)

    depth = GROUP * HD

    def product(cols, dtype):
        return pl.pallas_call(
            product_kernel,
            out_shape=jax.ShapeDtypeStruct((NX, rows, depth), dtype),
            grid_spec=pltpu.PrefetchScalarGridSpec(
                num_scalar_prefetch=1,
                grid=(NX,),
                in_specs=[
                    pl.BlockSpec((rows, depth), lambda i, cols: (0, 0)),
                    pl.BlockSpec((depth, depth), lambda i, cols: (0, cols[i])),
                ],
                out_specs=pl.BlockSpec((1, rows, depth), lambda i, cols: (i, 0, 0)),
            ),
            compiler_params=params(16),
            cost_estimate=cost(2),
            name="product",
        )(cols, attended, w_out)

    def small(kernel, count, shape, name, *operands):
        return pl.pallas_call(
            kernel,
            out_shape=[jax.ShapeDtypeStruct(shape, bf16)] * count,
            in_specs=[VSPEC] * len(operands),
            out_specs=[VSPEC] * count,
            compiler_params=params(16),
            cost_estimate=cost(0.4),
            name=name,
        )(*operands)

    away = product(away_cols, bf16)
    recv = swap_core(away)
    mine = product(home_cols, f32)
    upper, lower = small(halves_kernel, 2, (rows // 2, depth), "halves", mine, recv)
    upper, lower = shift_x(upper, 1), shift_x(lower, -1)
    right, left = small(pass_kernel, 2, (rows, depth), "pass", mine, recv, upper, lower)
    right, left = shift_x(right, 1), shift_x(left, -1)
    return small(final_kernel, 1, (rows, depth), "final", mine, recv, right, left)[0]


def solution(mesh):
    return jax.shard_map(
        local,
        mesh=mesh,
        in_specs=(
            P("seq", None),
            P(),
            P(None, "heads"),
            P(None, "heads"),
            P(None, "heads"),
            P("heads", None),
            P("heads", "seq", None),
            P("heads", "seq", None),
            P("heads", None),
            P("heads"),
            P("heads", None),
            P("heads"),
        ),
        out_specs=P("seq", "heads"),
        check_vma=False,
    )
```

time: 99.5 us -> 98.4 us (0.989)
  waiting for transfers between devices: 33.3 us -> 37.1 us
  local copies, waits for them, and re-layouts: 2.89 us -> 0.05 us
  Pallas kernels: 23.2 us -> 20.9 us
    ppermute x7, waiting for transfers between devices: 14 us -> 18.8 us  [shift_z(): lax.ppermute(block, 'seq', [(y * NZ + z, y * NZ + (z + d) % NZ) for y in...]
    unnamed x22 -> x18, local copies, waits for them, and re-layouts: 2.89 us -> 0.04 us
    pallas_call x10 -> x9, Pallas kernels: 15.8 us -> 14.2 us  [the longest x3 6.63 us: far(): pl.pallas_call(functools.partial(far_kernel, shift), out_shape=state_shap...]
    ppermute x9, waiting for transfers between devices: 6.65 us -> 5.19 us  [shift_y(): lax.ppermute(block, 'seq', [(y * NZ + z, (y + d) % NY * NZ + z) for y in...]
    ppermute x4, waiting for transfers between devices: 10.4 us -> 11.6 us  [shift_x(): lax.ppermute(block, 'heads', [(2 * x + c, 2 * ((x + d) % NX) + c) for x i...]
  transfers between devices with their start and end apart: 24 -> 23, of which waited for: 11 -> 13; matrix products, arithmetic and copies ran while one was open for 5% -> 4% of each run, Pallas kernels for 15% -> 11%
where the time goes in v3:
time: 98.4 us; the launch traced here: 98.1 us
  waiting for transfers between devices  37.1 us (38%)
  starting transfers between devices  32.8 us (33%)
  Pallas kernels  20.9 us (21%)
  other arithmetic  2.83 us (3%)
  matrix products  2.65 us (3%)
  between operations  1.71 us (2%)
    ppermute x7, waiting for transfers between devices, shift_z(): lax.ppermute(block, 'seq', [(y * NZ + z, y * NZ + (z + d) % NZ) for y in...  18.8 us
    ppermute x9, starting transfers between devices, shift_y(): lax.ppermute(block, 'seq', [(y * NZ + z, (y + d) % NY * NZ + z) for y in...  15.8 us
    ppermute x7, starting transfers between devices, shift_z(): lax.ppermute(block, 'seq', [(y * NZ + z, y * NZ + (z + d) % NZ) for y in...  12.8 us
    ppermute x4, waiting for transfers between devices, shift_x(): lax.ppermute(block, 'heads', [(2 * x + c, 2 * ((x + d) % NX) + c) for x i...  11.6 us
    pallas_call x3, Pallas kernels, far(): pl.pallas_call(functools.partial(far_kernel, shift), out_shape=state_shap...  6.63 us
    ppermute x9, waiting for transfers between devices, shift_y(): lax.ppermute(block, 'seq', [(y * NZ + z, (y + d) % NY * NZ + z) for y in...  5.19 us
    ppermute x4, starting transfers between devices, shift_x(): lax.ppermute(block, 'heads', [(2 * x + c, 2 * ((x + d) % NX) + c) for x i...  4.21 us
    pallas_call x2, Pallas kernels, product(): pl.pallas_call(product_kernel, out_shape=jax.ShapeDtypeStruct((NX, rows,...  3.94 us
  transfers between devices with their start and end apart: 23, of which 13 were waited for; matrix products, arithmetic and copies ran while one was open for 4% of the time, Pallas kernels for 11%

profile of v3, /device:TPU:6, one launch (start us, length us, event | category | flops | bytes accessed | tf_op | source)
XLA Modules:
  0.0 98.1 jit_solution(6612804229347576689)
XLA Ops:
  0.8 0.7 compare_select_fusion
  1.7 0.1 select_reduce_fusion
  1.8 0.6 compare_select_fusion.1.tab
  2.4 2.7 %pick.1 = (bf16[2,2,64,128]{3,2,1,0:T(8,128)(2,1)}, bf16[2,2,64,128]{3,2,1,0:T(8,128)(2,1)}, bf16[2,2,64,128]{3,2,1,0:T(8,128)(2,1)}, bf16[2,2,64,128]{3,2,1,0:T(8,128)(2,1)}) custom-call(s32[128]{0:T(128)} %compare_select_fusion.1.tab, bf16[1,1024,128]{2,1,0:T(8,128)(2,1)} %ck.1, bf16[1,1024,128]{2,1,0:T(8,128)(2,1)} %cv.1), custom_call_target="tpu_custom_call" | custom-call | flops 700000000 | tf_op jit(solution)/shard_map/pick/pallas_call | solution.py:298
  5.1 1.6 %collective-permute-start = (bf16[2,2,64,128]{3,2,1,0:T(8,128)(2,1)}, bf16[2,2,64,128]{3,2,1,0:T(8,128)(2,1)S(1)}, u32[]{:S(2)}, u32[]{:S(2)}) collective-permute-start(bf16[2,2,64,128]{3,2,1,0:T(8,128)(2,1)} %get-tuple-element.49), channel_id=1, source_target_pairs={{0,8},{1,9},{2,10},{3,11},{4,12},{5,13},{6,14},{7,15},{8,16},{9,17... | collective-permute-start | bytes 196616 | tf_op jit(solution)/shard_map/ppermute | solution.py:38
  6.7 2.9 %collective-permute-start.1 = (bf16[2,2,64,128]{3,2,1,0:T(8,128)(2,1)}, bf16[2,2,64,128]{3,2,1,0:T(8,128)(2,1)S(1)}, u32[]{:S(2)}, u32[]{:S(2)}) collective-permute-start(bf16[2,2,64,128]{3,2,1,0:T(8,128)(2,1)} %get-tuple-element.50), channel_id=1, source_target_pairs={{0,16},{1,17},{2,18},{3,19},{4,20},{5,21},{6,22},{7,23},{8,24},{9,... | collective-permute-start | bytes 196616 | tf_op jit(solution)/shard_map/ppermute | solution.py:38
  9.6 1.3 %collective-permute-start.2 = (bf16[2,2,64,128]{3,2,1,0:T(8,128)(2,1)}, bf16[2,2,64,128]{3,2,1,0:T(8,128)(2,1)S(1)}, u32[]{:S(2)}, u32[]{:S(2)}) collective-permute-start(bf16[2,2,64,128]{3,2,1,0:T(8,128)(2,1)} %get-tuple-element.51), channel_id=1, source_target_pairs={{0,24},{1,25},{2,26},{3,27},{4,28},{5,29},{6,30},{7,31},{8,0},{9,1... | collective-permute-start | bytes 196616 | tf_op jit(solution)/shard_map/ppermute | solution.py:38
  11.0 0.5 fusion
  11.5 0.7 fusion.2
  12.2 1.8 %collective-permute-done.2.r3 = bf16[2,2,64,128]{3,2,1,0:T(8,128)(2,1)S(1)} collective-permute-done((bf16[2,2,64,128]{3,2,1,0:T(8,128)(2,1)}, bf16[2,2,64,128]{3,2,1,0:T(8,128)(2,1)S(1)}, u32[]{:S(2)}, u32[]{:S(2)}) %collective-permute-start.2) | collective-permute-done | bytes 65568 | tf_op jit(solution)/shard_map/ppermute | solution.py:38
  14.1 0.8 column.1.refs_0_
  14.9 6.0 %collective-permute-start.9 = (bf16[8,2,64,128]{3,2,1,0:T(8,128)(2,1)S(1)}, bf16[8,2,64,128]{3,2,1,0:T(8,128)(2,1)S(1)}, u32[]{:S(2)}, u32[]{:S(2)}) collective-permute-start(bf16[8,2,64,128]{3,2,1,0:T(8,128)(2,1)S(1)} %column.1.refs_0_), channel_id=1, source_target_pairs={{0,7},{1,0},{2,1},{3,2},{4,3},{5,4},{6,5},{7,6},{8,15},{9,8},{10,9... | collective-permute-start | bytes 786440 | tf_op jit(solution)/shard_map/ppermute | solution.py:44
  20.9 0.7 convolution_convert_fusion.1.v
  21.6 0.7 convolution_convert_fusion.2.k
  22.4 6.1 %collective-permute-done.3.refs_1_ = bf16[8,2,64,128]{3,2,1,0:T(8,128)(2,1)S(1)} collective-permute-done((bf16[8,2,64,128]{3,2,1,0:T(8,128)(2,1)S(1)}, bf16[8,2,64,128]{3,2,1,0:T(8,128)(2,1)S(1)}, u32[]{:S(2)}, u32[]{:S(2)}) %collective-permute-start.3) | collective-permute-done | bytes 262176 | tf_op jit(solution)/shard_map/ppermute | solution.py:44
  28.5 1.2 %convolution_convert_fusion.q = bf16[256,512]{1,0:T(8,128)(2,1)S(1)} fusion(bf16[256,4096]{1,0:T(8,128)(2,1)S(1)} %fusion.2, bf16[4096,512]{1,0:T(8,128)(2,1)S(1)} %copy-done.8), kind=kOutput, calls=%fused_computation.5 | convolution fusion | flops 1073872896 | bytes 6553600 | tf_op jit(solution)/shard_map/dot_general | solution.py:334
  29.7 6.6 %collective-permute-done.4.refs_2_ = bf16[8,2,64,128]{3,2,1,0:T(8,128)(2,1)S(1)} collective-permute-done((bf16[8,2,64,128]{3,2,1,0:T(8,128)(2,1)S(1)}, bf16[8,2,64,128]{3,2,1,0:T(8,128)(2,1)S(1)}, u32[]{:S(2)}, u32[]{:S(2)}) %collective-permute-start.4) | collective-permute-done | bytes 262176 | tf_op jit(solution)/shard_map/ppermute | solution.py:44
  36.4 3.2 %collective-permute-start.10 = (bf16[8,2,64,128]{3,2,1,0:T(8,128)(2,1)S(1)}, bf16[8,2,64,128]{3,2,1,0:T(8,128)(2,1)S(1)}, u32[]{:S(2)}, u32[]{:S(2)}) collective-permute-start(bf16[8,2,64,128]{3,2,1,0:T(8,128)(2,1)S(1)} %collective-permute-done.9.refs_7_), channel_id=1, source_target_pairs={{0,7},{1,0},{2,1},{3,2},{4,3},{5,4},{6,5},{7,6},{8,15},{9,8},{10,9... | collective-permute-start | bytes 786440 | tf_op jit(solution)/shard_map/ppermute | solution.py:44
  39.6 5.7 %collective-permute-done.5.refs_3_ = bf16[8,2,64,128]{3,2,1,0:T(8,128)(2,1)S(1)} collective-permute-done((bf16[8,2,64,128]{3,2,1,0:T(8,128)(2,1)S(1)}, bf16[8,2,64,128]{3,2,1,0:T(8,128)(2,1)S(1)}, u32[]{:S(2)}, u32[]{:S(2)}) %collective-permute-start.5) | collective-permute-done | bytes 262176 | tf_op jit(solution)/shard_map/ppermute | solution.py:44
  45.3 3.6 %collective-permute-start.11 = (bf16[8,2,64,128]{3,2,1,0:T(8,128)(2,1)S(1)}, bf16[8,2,64,128]{3,2,1,0:T(8,128)(2,1)S(1)}, u32[]{:S(2)}, u32[]{:S(2)}) collective-permute-start(bf16[8,2,64,128]{3,2,1,0:T(8,128)(2,1)S(1)} %collective-permute-done.10.refs_6_), channel_id=1, source_target_pairs={{0,7},{1,0},{2,1},{3,2},{4,3},{5,4},{6,5},{7,6},{8,15},{9,8},{10,9... | collective-permute-start | bytes 786440 | tf_op jit(solution)/shard_map/ppermute | solution.py:44
  49.5 0.8 collective-permute-done.8.vp
  50.3 2.2 %near.1 = (f32[4,256,128]{2,1,0:T(8,128)S(1)}, f32[4,256,128]{2,1,0:T(8,128)S(1)}, f32[4,256,128]{2,1,0:T(8,128)S(1)}) custom-call(s32[1,4]{1,0:T(1,128)S(1)} %copy-done.2, s32[1]{0:T(128)S(6)} %copy.14.cnt, bf16[256,512]{1,0:T(8,128)(2,1)S(1)} %convolution_convert_fusion.q, bf16[256,128]{1,0:T(8,128)(2,1)S(1)} %collective-permute-done.7.kp, ...), custom_call_target="tpu_custom_call" | custom-call | flops 2200000000 | tf_op jit(solution)/shard_map/near/pallas_call | solution.py:338
  52.5 0.4 collective-permute-done.6.refs_4_
  52.9 1.4 %row.1 = (bf16[2,512,128]{2,1,0:T(8,128)(2,1)S(1)}, bf16[2,512,128]{2,1,0:T(8,128)(2,1)S(1)}) custom-call(s32[128]{0:T(128)S(1)} %copy-done.3, bf16[8,2,64,128]{3,2,1,0:T(8,128)(2,1)S(1)} %column.1.refs_0_, bf16[8,2,64,128]{3,2,1,0:T(8,128)(2,1)S(1)} %collective-permute-done.3.refs_1_, bf16[8,2,64,128]{3,2,1,0:T(8,128)(2,1)S(1)} %collective-permute-done.4.refs_2_, ...), custom_call_target="tpu_custom_call" | custom-call | flops 1300000000 | tf_op jit(solution)/shard_map/row/pallas_call | solution.py:350
  54.3 0.7 collective-permute-start.12
  55.0 2.6 %collective-permute-start.14 = (bf16[2,512,128]{2,1,0:T(8,128)(2,1)S(1)}, bf16[2,512,128]{2,1,0:T(8,128)(2,1)S(1)}, u32[]{:S(2)}, u32[]{:S(2)}) collective-permute-start(bf16[2,512,128]{2,1,0:T(8,128)(2,1)S(1)} %get-tuple-element.72.hi), channel_id=1, source_target_pairs={{0,24},{1,25},{2,26},{3,27},{4,28},{5,29},{6,30},{7,31},{8,0},{9,1... | collective-permute-start | bytes 786440 | tf_op jit(solution)/shard_map/ppermute | solution.py:38
  57.6 2.2 %far.3 = (f32[4,256,128]{2,1,0:T(8,128)S(1)}, f32[4,256,128]{2,1,0:T(8,128)S(1)}, f32[4,256,128]{2,1,0:T(8,128)S(1)}) custom-call(s32[128]{0:T(128)S(1)} %copy-done.3, bf16[256,512]{1,0:T(8,128)(2,1)S(1)} %convolution_convert_fusion.q, bf16[2,512,128]{2,1,0:T(8,128)(2,1)S(1)} %get-tuple-element.71.lo, bf16[2,512,128]{2,1,0:T(8,128)(2,1)S(1)} %get-tuple-element.72.hi, ...), custom_call_target="tpu_custom_call" | custom-call | flops 1800000000 | tf_op jit(solution)/shard_map/far/pallas_call | solution.py:360
  59.9 3.2 %collective-permute-start.16 = (bf16[2,512,128]{2,1,0:T(8,128)(2,1)S(1)}, bf16[2,512,128]{2,1,0:T(8,128)(2,1)S(1)}, u32[]{:S(2)}, u32[]{:S(2)}) collective-permute-start(bf16[2,512,128]{2,1,0:T(8,128)(2,1)S(1)} %get-tuple-element.71.lo), channel_id=1, source_target_pairs={{0,24},{1,25},{2,26},{3,27},{4,28},{5,29},{6,30},{7,31},{8,0},{9,1... | collective-permute-start | bytes 786440 | tf_op jit(solution)/shard_map/ppermute | solution.py:38
  63.1 1.6 %collective-permute-done.12.lo = bf16[2,512,128]{2,1,0:T(8,128)(2,1)S(1)} collective-permute-done((bf16[2,512,128]{2,1,0:T(8,128)(2,1)S(1)}, bf16[2,512,128]{2,1,0:T(8,128)(2,1)S(1)}, u32[]{:S(2)}, u32[]{:S(2)}) %collective-permute-start.12) | collective-permute-done | bytes 262176 | tf_op jit(solution)/shard_map/ppermute | solution.py:38
  64.7 3.3 %collective-permute-start.15 = (bf16[2,512,128]{2,1,0:T(8,128)(2,1)S(1)}, bf16[2,512,128]{2,1,0:T(8,128)(2,1)S(1)}, u32[]{:S(2)}, u32[]{:S(2)}) collective-permute-start(bf16[2,512,128]{2,1,0:T(8,128)(2,1)S(1)} %collective-permute-done.14.hi), channel_id=1, source_target_pairs={{0,24},{1,25},{2,26},{3,27},{4,28},{5,29},{6,30},{7,31},{8,0},{9,1... | collective-permute-start | bytes 786440 | tf_op jit(solution)/shard_map/ppermute | solution.py:38
  68.0 1.8 %collective-permute-done.17.hi = bf16[2,512,128]{2,1,0:T(8,128)(2,1)S(1)} collective-permute-done((bf16[2,512,128]{2,1,0:T(8,128)(2,1)S(1)}, bf16[2,512,128]{2,1,0:T(8,128)(2,1)S(1)}, u32[]{:S(2)}, u32[]{:S(2)}) %collective-permute-start.17) | collective-permute-done | bytes 262176 | tf_op jit(solution)/shard_map/ppermute | solution.py:38
  69.7 2.2 %far.4 = (f32[4,256,128]{2,1,0:T(8,128)S(1)}, f32[4,256,128]{2,1,0:T(8,128)S(1)}, f32[4,256,128]{2,1,0:T(8,128)S(1)}) custom-call(s32[128]{0:T(128)S(1)} %copy-done.3, bf16[256,512]{1,0:T(8,128)(2,1)S(1)} %convolution_convert_fusion.q, bf16[2,512,128]{2,1,0:T(8,128)(2,1)S(1)} %collective-permute-done.12.lo, ...), custom_call_target="tpu_custom_call" | custom-call | flops 1800000000 | tf_op jit(solution)/shard_map/far/pallas_call | solution.py:360
  71.9 2.2 %far.5 = (f32[4,256,128]{2,1,0:T(8,128)S(1)}, f32[4,256,128]{2,1,0:T(8,128)S(1)}, f32[4,256,128]{2,1,0:T(8,128)S(1)}) custom-call(s32[128]{0:T(128)S(1)} %copy-done.3, bf16[256,512]{1,0:T(8,128)(2,1)S(1)} %convolution_convert_fusion.q, bf16[2,512,128]{2,1,0:T(8,128)(2,1)S(1)} %collective-permute-done.16.lo, ...), custom_call_target="tpu_custom_call" | custom-call | flops 1800000000 | tf_op jit(solution)/shard_map/far/pallas_call | solution.py:360
  74.2 2.3 %last.1.att = bf16[256,512]{1,0:T(8,128)(2,1)S(1)} custom-call(s32[128]{0:T(128)S(1)} %copy-done.3, bf16[256,512]{1,0:T(8,128)(2,1)S(1)} %convolution_convert_fusion.q, bf16[2,512,128]{2,1,0:T(8,128)(2,1)S(1)} %collective-permute-done.13.lo, bf16[2,512,128]{2,1,0:T(8,128)(2,1)S(1)} %collective-permute-done.15.hi, f32[4,256,128]{2,1,0:T(8,128)S(1)} %get-tuple-element.79.m_in, ...), custom_call_target="tpu_custom_call" | custom-call | flops 2500000000 | tf_op jit(solution)/shard_map/last/pallas_call | solution.py:376
  76.5 2.0 %product.3 = bf16[4,256,512]{2,1,0:T(8,128)(2,1)S(1)} custom-call(s32[4]{0:T(128)S(1)} %get-tuple-element.82.cols, bf16[256,512]{1,0:T(8,128)(2,1)S(1)} %last.1.att, bf16[512,4096]{1,0:T(8,128)(2,1)S(1)} %copy-done.1), custom_call_target="tpu_custom_call" | custom-call | flops 2000000000 | tf_op jit(solution)/shard_map/product/pallas_call | solution.py:389
  78.5 0.1 collective-permute-start.18
  78.6 2.0 %product.2.mine = f32[4,256,512]{2,1,0:T(8,128)S(1)} custom-call(s32[4]{0:T(128)S(1)} %get-tuple-element.46.cols, bf16[256,512]{1,0:T(8,128)(2,1)S(1)} %last.1.att, bf16[512,4096]{1,0:T(8,128)(2,1)S(1)} %copy-done.1), custom_call_target="tpu_custom_call" | custom-call | flops 2000000000 | tf_op jit(solution)/shard_map/product/pallas_call | solution.py:389
  80.6 0.7 collective-permute-done.18.recv
  81.3 0.6 collective-permute-start.19
  81.9 1.5 %collective-permute-start.20 = (bf16[128,512]{1,0:T(8,128)(2,1)S(1)}, bf16[128,512]{1,0:T(8,128)(2,1)S(1)}, u32[]{:S(2)}, u32[]{:S(2)}) collective-permute-start(bf16[128,512]{1,0:T(8,128)(2,1)S(1)} %get-tuple-element.84), channel_id=1, source_target_pairs={{0,192},{32,224},{64,0},{96,32},{128,64},{160,96},{192,128},{224,1... | collective-permute-start | bytes 393224 | tf_op jit(solution)/shard_map/ppermute | solution.py:50
  83.4 3.5 %collective-permute-done.19.a = bf16[128,512]{1,0:T(8,128)(2,1)S(1)} collective-permute-done((bf16[128,512]{1,0:T(8,128)(2,1)S(1)}, bf16[128,512]{1,0:T(8,128)(2,1)S(1)}, u32[]{:S(2)}, u32[]{:S(2)}) %collective-permute-start.19) | collective-permute-done | bytes 131104 | tf_op jit(solution)/shard_map/ppermute | solution.py:50
  86.9 1.4 %collective-permute-done.20.b = bf16[128,512]{1,0:T(8,128)(2,1)S(1)} collective-permute-done((bf16[128,512]{1,0:T(8,128)(2,1)S(1)}, bf16[128,512]{1,0:T(8,128)(2,1)S(1)}, u32[]{:S(2)}, u32[]{:S(2)}) %collective-permute-start.20) | collective-permute-done | bytes 131104 | tf_op jit(solution)/shard_map/ppermute | solution.py:50
  88.3 0.1 pass.1
  88.5 0.4 collective-permute-start.21
  88.8 1.7 %collective-permute-start.22 = (bf16[256,512]{1,0:T(8,128)(2,1)S(1)}, bf16[256,512]{1,0:T(8,128)(2,1)S(1)}, u32[]{:S(2)}, u32[]{:S(2)}) collective-permute-start(bf16[256,512]{1,0:T(8,128)(2,1)S(1)} %get-tuple-element.86), channel_id=1, source_target_pairs={{0,192},{32,224},{64,0},{96,32},{128,64},{160,96},{192,128},{224,1... | collective-permute-start | bytes 786440 | tf_op jit(solution)/shard_map/ppermute | solution.py:50
  90.6 5.2 %collective-permute-done.21.a = bf16[256,512]{1,0:T(8,128)(2,1)S(1)} collective-permute-done((bf16[256,512]{1,0:T(8,128)(2,1)S(1)}, bf16[256,512]{1,0:T(8,128)(2,1)S(1)}, u32[]{:S(2)}, u32[]{:S(2)}) %collective-permute-start.21) | collective-permute-done | bytes 262176 | tf_op jit(solution)/shard_map/ppermute | solution.py:50
  95.7 1.5 %collective-permute-done.22.b = bf16[256,512]{1,0:T(8,128)(2,1)S(1)} collective-permute-done((bf16[256,512]{1,0:T(8,128)(2,1)S(1)}, bf16[256,512]{1,0:T(8,128)(2,1)S(1)}, u32[]{:S(2)}, u32[]{:S(2)}) %collective-permute-start.22) | collective-permute-done | bytes 262176 | tf_op jit(solution)/shard_map/ppermute | solution.py:50
  97.3 0.8 final.1
  (43 shorter events, 0.4 us)
Async XLA Ops:
  0.0 20.9 %copy-start = (bf16[4096,128]{1,0:T(8,128)(2,1)S(1)}, bf16[4096,128]{1,0:T(8,128)(2,1)}, u32[]{:S(2)}) copy-start(bf16[4096,128]{1,0:T(8,128)(2,1)} %param.16) | copy-start | bytes 3145732
  0.0 10.9 %copy-start.5 = (bf16[256,4096]{1,0:T(8,128)(2,1)S(1)}, bf16[256,4096]{1,0:T(8,128)(2,1)}, u32[]{:S(2)}) copy-start(bf16[256,4096]{1,0:T(8,128)(2,1)} %param.12) | copy-start | bytes 6291460
  2.4 9.0 %copy-start.7 = (f32[4096]{0:T(1024)S(1)}, f32[4096]{0:T(1024)}, u32[]{:S(2)}) copy-start(f32[4096]{0:T(1024)} %param.13) | copy-start | bytes 49156
  5.1 9.0 %collective-permute-start = (bf16[2,2,64,128]{3,2,1,0:T(8,128)(2,1)}, bf16[2,2,64,128]{3,2,1,0:T(8,128)(2,1)S(1)}, u32[]{:S(2)}, u32[]{:S(2)}) collective-permute-start(bf16[2,2,64,128]{3,2,1,0:T(8,128)(2,1)} %get-tuple-element.49), channel_id=1, source_target_pairs={{0,8},{1,9},{2,10},{3,11},{4,12},{5,13},{6,14},{7,15},{8,16},{9,17... | collective-permute-start | bytes 196616 | tf_op jit(solution)/shard_map/ppermute | solution.py:38
  6.7 7.4 %collective-permute-start.1 = (bf16[2,2,64,128]{3,2,1,0:T(8,128)(2,1)}, bf16[2,2,64,128]{3,2,1,0:T(8,128)(2,1)S(1)}, u32[]{:S(2)}, u32[]{:S(2)}) collective-permute-start(bf16[2,2,64,128]{3,2,1,0:T(8,128)(2,1)} %get-tuple-element.50), channel_id=1, source_target_pairs={{0,16},{1,17},{2,18},{3,19},{4,20},{5,21},{6,22},{7,23},{8,24},{9,... | collective-permute-start | bytes 196616 | tf_op jit(solution)/shard_map/ppermute | solution.py:38
  9.6 4.5 %collective-permute-start.2 = (bf16[2,2,64,128]{3,2,1,0:T(8,128)(2,1)}, bf16[2,2,64,128]{3,2,1,0:T(8,128)(2,1)S(1)}, u32[]{:S(2)}, u32[]{:S(2)}) collective-permute-start(bf16[2,2,64,128]{3,2,1,0:T(8,128)(2,1)} %get-tuple-element.51), channel_id=1, source_target_pairs={{0,24},{1,25},{2,26},{3,27},{4,28},{5,29},{6,30},{7,31},{8,0},{9,1... | collective-permute-start | bytes 196616 | tf_op jit(solution)/shard_map/ppermute | solution.py:38
  11.5 2.6 %copy-start.3 = (s32[128]{0:T(128)S(1)}, s32[128]{0:T(128)}, u32[]{:S(2)}) copy-start(s32[128]{0:T(128)} %compare_select_fusion.1.tab) | copy-start | bytes 1540
  11.5 2.6 %copy-start.4 = (bf16[2,2,64,128]{3,2,1,0:T(8,128)(2,1)S(1)}, bf16[2,2,64,128]{3,2,1,0:T(8,128)(2,1)}, u32[]{:S(2)}) copy-start(bf16[2,2,64,128]{3,2,1,0:T(8,128)(2,1)} %get-tuple-element.48.r0) | copy-start | bytes 196612
  14.9 6.7 %copy-start.6 = (bf16[4096,128]{1,0:T(8,128)(2,1)S(1)}, bf16[4096,128]{1,0:T(8,128)(2,1)}, u32[]{:S(2)}) copy-start(bf16[4096,128]{1,0:T(8,128)(2,1)} %param.15) | copy-start | bytes 3145732
  14.9 21.4 %collective-permute-start.9 = (bf16[8,2,64,128]{3,2,1,0:T(8,128)(2,1)S(1)}, bf16[8,2,64,128]{3,2,1,0:T(8,128)(2,1)S(1)}, u32[]{:S(2)}, u32[]{:S(2)}) collective-permute-start(bf16[8,2,64,128]{3,2,1,0:T(8,128)(2,1)S(1)} %column.1.refs_0_), channel_id=1, source_target_pairs={{0,7},{1,0},{2,1},{3,2},{4,3},{5,4},{6,5},{7,6},{8,15},{9,8},{10,9... | collective-permute-start | bytes 786440 | tf_op jit(solution)/shard_map/ppermute | solution.py:44
  20.9 7.6 %collective-permute-start.3 = (bf16[8,2,64,128]{3,2,1,0:T(8,128)(2,1)S(1)}, bf16[8,2,64,128]{3,2,1,0:T(8,128)(2,1)S(1)}, u32[]{:S(2)}, u32[]{:S(2)}) collective-permute-start(bf16[8,2,64,128]{3,2,1,0:T(8,128)(2,1)S(1)} %column.1.refs_0_), channel_id=1, source_target_pairs={{0,1},{1,2},{2,3},{3,4},{4,5},{5,6},{6,7},{7,0},{8,9},{9,10},{10,1... | collective-permute-start | bytes 786440 | tf_op jit(solution)/shard_map/ppermute | solution.py:44
  20.9 7.6 %copy-start.8 = (bf16[4096,512]{1,0:T(8,128)(2,1)S(1)}, bf16[4096,512]{1,0:T(8,128)(2,1)}, u32[]{:S(2)}) copy-start(bf16[4096,512]{1,0:T(8,128)(2,1)} %param.14) | copy-start | bytes 12582916
  22.3 28.0 %copy-start.2 = (s32[1,4]{1,0:T(1,128)S(1)}, s32[1,4]{1,0:T(1,128)}, u32[]{:S(2)}) copy-start(s32[1,4]{1,0:T(1,128)} %offs.1) | copy-start | bytes 52
  28.5 7.9 %collective-permute-start.4 = (bf16[8,2,64,128]{3,2,1,0:T(8,128)(2,1)S(1)}, bf16[8,2,64,128]{3,2,1,0:T(8,128)(2,1)S(1)}, u32[]{:S(2)}, u32[]{:S(2)}) collective-permute-start(bf16[8,2,64,128]{3,2,1,0:T(8,128)(2,1)S(1)} %collective-permute-done.3.refs_1_), channel_id=1, source_target_pairs={{0,1},{1,2},{2,3},{3,4},{4,5},{5,6},{6,7},{7,0},{8,9},{9,10},{10,1... | collective-permute-start | bytes 786440 | tf_op jit(solution)/shard_map/ppermute | solution.py:44
  36.4 9.0 %collective-permute-start.5 = (bf16[8,2,64,128]{3,2,1,0:T(8,128)(2,1)S(1)}, bf16[8,2,64,128]{3,2,1,0:T(8,128)(2,1)S(1)}, u32[]{:S(2)}, u32[]{:S(2)}) collective-permute-start(bf16[8,2,64,128]{3,2,1,0:T(8,128)(2,1)S(1)} %collective-permute-done.4.refs_2_), channel_id=1, source_target_pairs={{0,1},{1,2},{2,3},{3,4},{4,5},{5,6},{6,7},{7,0},{8,9},{9,10},{10,1... | collective-permute-start | bytes 786440 | tf_op jit(solution)/shard_map/ppermute | solution.py:44
  36.4 9.0 %collective-permute-start.10 = (bf16[8,2,64,128]{3,2,1,0:T(8,128)(2,1)S(1)}, bf16[8,2,64,128]{3,2,1,0:T(8,128)(2,1)S(1)}, u32[]{:S(2)}, u32[]{:S(2)}) collective-permute-start(bf16[8,2,64,128]{3,2,1,0:T(8,128)(2,1)S(1)} %collective-permute-done.9.refs_7_), channel_id=1, source_target_pairs={{0,7},{1,0},{2,1},{3,2},{4,3},{5,4},{6,5},{7,6},{8,15},{9,8},{10,9... | collective-permute-start | bytes 786440 | tf_op jit(solution)/shard_map/ppermute | solution.py:44
  39.6 9.9 %collective-permute-start.7 = (bf16[256,128]{1,0:T(8,128)(2,1)S(1)}, bf16[256,128]{1,0:T(8,128)(2,1)S(1)}, u32[]{:S(2)}, u32[]{:S(2)}) collective-permute-start(bf16[256,128]{1,0:T(8,128)(2,1)S(1)} %convolution_convert_fusion.2.k), channel_id=1, source_target_pairs={{0,1},{1,2},{2,3},{3,4},{4,5},{5,6},{6,7},{7,8},{8,9},{9,10},{10,1... | collective-permute-start | bytes 196616 | tf_op jit(solution)/shard_map/ppermute | solution.py:333
  39.6 10.7 %collective-permute-start.8 = (bf16[256,128]{1,0:T(8,128)(2,1)S(1)}, bf16[256,128]{1,0:T(8,128)(2,1)S(1)}, u32[]{:S(2)}, u32[]{:S(2)}) collective-permute-start(bf16[256,128]{1,0:T(8,128)(2,1)S(1)} %convolution_convert_fusion.1.v), channel_id=1, source_target_pairs={{0,1},{1,2},{2,3},{3,4},{4,5},{5,6},{6,7},{7,8},{8,9},{9,10},{10,1... | collective-permute-start | bytes 196616 | tf_op jit(solution)/shard_map/ppermute | solution.py:333
  45.3 7.6 %collective-permute-start.6 = (bf16[8,2,64,128]{3,2,1,0:T(8,128)(2,1)S(1)}, bf16[8,2,64,128]{3,2,1,0:T(8,128)(2,1)S(1)}, u32[]{:S(2)}, u32[]{:S(2)}) collective-permute-start(bf16[8,2,64,128]{3,2,1,0:T(8,128)(2,1)S(1)} %collective-permute-done.5.refs_3_), channel_id=1, source_target_pairs={{0,1},{1,2},{2,3},{3,4},{4,5},{5,6},{6,7},{7,0},{8,9},{9,10},{10,1... | collective-permute-start | bytes 786440 | tf_op jit(solution)/shard_map/ppermute | solution.py:44
  45.3 7.6 %collective-permute-start.11 = (bf16[8,2,64,128]{3,2,1,0:T(8,128)(2,1)S(1)}, bf16[8,2,64,128]{3,2,1,0:T(8,128)(2,1)S(1)}, u32[]{:S(2)}, u32[]{:S(2)}) collective-permute-start(bf16[8,2,64,128]{3,2,1,0:T(8,128)(2,1)S(1)} %collective-permute-done.10.refs_6_), channel_id=1, source_target_pairs={{0,7},{1,0},{2,1},{3,2},{4,3},{5,4},{6,5},{7,6},{8,15},{9,8},{10,9... | collective-permute-start | bytes 786440 | tf_op jit(solution)/shard_map/ppermute | solution.py:44
  54.3 10.4 %collective-permute-start.12 = (bf16[2,512,128]{2,1,0:T(8,128)(2,1)S(1)}, bf16[2,512,128]{2,1,0:T(8,128)(2,1)S(1)}, u32[]{:S(2)}, u32[]{:S(2)}) collective-permute-start(bf16[2,512,128]{2,1,0:T(8,128)(2,1)S(1)} %get-tuple-element.71.lo), channel_id=1, source_target_pairs={{0,8},{1,9},{2,10},{3,11},{4,12},{5,13},{6,14},{7,15},{8,16},{9,17... | collective-permute-start | bytes 786440 | tf_op jit(solution)/shard_map/ppermute | solution.py:38
  55.0 9.7 %collective-permute-start.14 = (bf16[2,512,128]{2,1,0:T(8,128)(2,1)S(1)}, bf16[2,512,128]{2,1,0:T(8,128)(2,1)S(1)}, u32[]{:S(2)}, u32[]{:S(2)}) collective-permute-start(bf16[2,512,128]{2,1,0:T(8,128)(2,1)S(1)} %get-tuple-element.72.hi), channel_id=1, source_target_pairs={{0,24},{1,25},{2,26},{3,27},{4,28},{5,29},{6,30},{7,31},{8,0},{9,1... | collective-permute-start | bytes 786440 | tf_op jit(solution)/shard_map/ppermute | solution.py:38
  59.8 9.9 %collective-permute-start.17 = (bf16[2,512,128]{2,1,0:T(8,128)(2,1)S(1)}, bf16[2,512,128]{2,1,0:T(8,128)(2,1)S(1)}, u32[]{:S(2)}, u32[]{:S(2)}) collective-permute-start(bf16[2,512,128]{2,1,0:T(8,128)(2,1)S(1)} %get-tuple-element.72.hi), channel_id=1, source_target_pairs={{0,8},{1,9},{2,10},{3,11},{4,12},{5,13},{6,14},{7,15},{8,16},{9,17... | collective-permute-start | bytes 786440 | tf_op jit(solution)/shard_map/ppermute | solution.py:38
  59.9 12.0 %collective-permute-start.16 = (bf16[2,512,128]{2,1,0:T(8,128)(2,1)S(1)}, bf16[2,512,128]{2,1,0:T(8,128)(2,1)S(1)}, u32[]{:S(2)}, u32[]{:S(2)}) collective-permute-start(bf16[2,512,128]{2,1,0:T(8,128)(2,1)S(1)} %get-tuple-element.71.lo), channel_id=1, source_target_pairs={{0,24},{1,25},{2,26},{3,27},{4,28},{5,29},{6,30},{7,31},{8,0},{9,1... | collective-permute-start | bytes 786440 | tf_op jit(solution)/shard_map/ppermute | solution.py:38
  64.7 9.5 %collective-permute-start.13 = (bf16[2,512,128]{2,1,0:T(8,128)(2,1)S(1)}, bf16[2,512,128]{2,1,0:T(8,128)(2,1)S(1)}, u32[]{:S(2)}, u32[]{:S(2)}) collective-permute-start(bf16[2,512,128]{2,1,0:T(8,128)(2,1)S(1)} %collective-permute-done.12.lo), channel_id=1, source_target_pairs={{0,8},{1,9},{2,10},{3,11},{4,12},{5,13},{6,14},{7,15},{8,16},{9,17... | collective-permute-start | bytes 786440 | tf_op jit(solution)/shard_map/ppermute | solution.py:38
  64.7 9.5 %collective-permute-start.15 = (bf16[2,512,128]{2,1,0:T(8,128)(2,1)S(1)}, bf16[2,512,128]{2,1,0:T(8,128)(2,1)S(1)}, u32[]{:S(2)}, u32[]{:S(2)}) collective-permute-start(bf16[2,512,128]{2,1,0:T(8,128)(2,1)S(1)} %collective-permute-done.14.hi), channel_id=1, source_target_pairs={{0,24},{1,25},{2,26},{3,27},{4,28},{5,29},{6,30},{7,31},{8,0},{9,1... | collective-permute-start | bytes 786440 | tf_op jit(solution)/shard_map/ppermute | solution.py:38
  74.2 2.3 %copy-start.1 = (bf16[512,4096]{1,0:T(8,128)(2,1)S(1)}, bf16[512,4096]{1,0:T(8,128)(2,1)}, u32[]{:S(2)}) copy-start(bf16[512,4096]{1,0:T(8,128)(2,1)} %w.3) | copy-start | bytes 12582916
  78.5 2.7 %collective-permute-start.18 = (bf16[4,256,512]{2,1,0:T(8,128)(2,1)S(1)}, bf16[4,256,512]{2,1,0:T(8,128)(2,1)S(1)}, u32[]{:S(2)}, u32[]{:S(2)}) collective-permute-start(bf16[4,256,512]{2,1,0:T(8,128)(2,1)S(1)} %product.3), channel_id=1, source_target_pairs={{0,32},{32,0},{64,96},{96,64},{128,160},{160,128},{192,224},{224,1... | collective-permute-start | bytes 3145736 | tf_op jit(solution)/shard_map/ppermute | solution.py:56
  81.3 5.6 %collective-permute-start.19 = (bf16[128,512]{1,0:T(8,128)(2,1)S(1)}, bf16[128,512]{1,0:T(8,128)(2,1)S(1)}, u32[]{:S(2)}, u32[]{:S(2)}) collective-permute-start(bf16[128,512]{1,0:T(8,128)(2,1)S(1)} %get-tuple-element.83), channel_id=1, source_target_pairs={{0,64},{32,96},{64,128},{96,160},{128,192},{160,224},{192,0},{224,... | collective-permute-start | bytes 393224 | tf_op jit(solution)/shard_map/ppermute | solution.py:50
  81.9 6.5 %collective-permute-start.20 = (bf16[128,512]{1,0:T(8,128)(2,1)S(1)}, bf16[128,512]{1,0:T(8,128)(2,1)S(1)}, u32[]{:S(2)}, u32[]{:S(2)}) collective-permute-start(bf16[128,512]{1,0:T(8,128)(2,1)S(1)} %get-tuple-element.84), channel_id=1, source_target_pairs={{0,192},{32,224},{64,0},{96,32},{128,64},{160,96},{192,128},{224,1... | collective-permute-start | bytes 393224 | tf_op jit(solution)/shard_map/ppermute | solution.py:50
  88.5 7.3 %collective-permute-start.21 = (bf16[256,512]{1,0:T(8,128)(2,1)S(1)}, bf16[256,512]{1,0:T(8,128)(2,1)S(1)}, u32[]{:S(2)}, u32[]{:S(2)}) collective-permute-start(bf16[256,512]{1,0:T(8,128)(2,1)S(1)} %get-tuple-element.85), channel_id=1, source_target_pairs={{0,64},{32,96},{64,128},{96,160},{128,192},{160,224},{192,0},{224,... | collective-permute-start | bytes 786440 | tf_op jit(solution)/shard_map/ppermute | solution.py:50
  88.8 8.5 %collective-permute-start.22 = (bf16[256,512]{1,0:T(8,128)(2,1)S(1)}, bf16[256,512]{1,0:T(8,128)(2,1)S(1)}, u32[]{:S(2)}, u32[]{:S(2)}) collective-permute-start(bf16[256,512]{1,0:T(8,128)(2,1)S(1)} %get-tuple-element.86), channel_id=1, source_target_pairs={{0,192},{32,224},{64,0},{96,32},{128,64},{160,96},{192,128},{224,1... | collective-permute-start | bytes 786440 | tf_op jit(solution)/shard_map/ppermute | solution.py:50
